TPU v7x, 128 devices: a whole 4x4x4 slice. The times are simulated.
128 devices in a mesh: batch: 8 (over x, core), feat: 16 (over y, z).
Axes of the slice: x: 4, y: 4, z: 4, core: 2. Of those that a mesh axis runs over, the one named last changes fastest.
Arguments:
- view_a: bfloat16 [4096, 8192], P('batch', 'feat'), may hold values from -800 to 800
- view_b: bfloat16 [4096, 8192], P('batch', 'feat'), may hold values from -800 to 800
Outputs:
- grad_a: bfloat16 [4096, 8192], P('batch', 'feat')
- grad_b: bfloat16 [4096, 8192], P('batch', 'feat')
All inputs are finite; a program needn't handle non-finite values.
Results may differ from a plain program's by a relative error of at most 0.0069.
Values may be sent and summed in bfloat16 or wider, within the bound.
A program may use at most 128 MiB of HBM per device.

v0:
```python
import jax
import jax.numpy as jnp
from jax import lax
from jax.sharding import PartitionSpec as P


def penalize(corr, row_first):
    rows_here = row_first + lax.broadcasted_iota(jnp.int32, corr.shape, 0)
    cols_here = lax.broadcasted_iota(jnp.int32, corr.shape, 1)
    return jnp.where(rows_here == cols_here, 2.0 * (corr - 1.0), 2.0 * 0.0051 * corr).astype(
        jnp.bfloat16
    )


def backward(back, unit, scales, first_sum, second_sum, total):
    return (scales * (back - first_sum / total - unit * (second_sum / total))).astype(jnp.bfloat16)


def body(view_a, view_b):
    rows_dev, width = view_a.shape
    total = rows_dev * lax.axis_size("batch")
    values_a = view_a.astype(jnp.float32)
    values_b = view_b.astype(jnp.float32)
    sum_a, square_a, sum_b, square_b = lax.psum(
        (
            jnp.sum(values_a, axis=0),
            jnp.sum(values_a * values_a, axis=0),
            jnp.sum(values_b, axis=0),
            jnp.sum(values_b * values_b, axis=0),
        ),
        "batch",
    )
    mean_a = sum_a / total
    mean_b = sum_b / total
    scales_a = lax.rsqrt(square_a / total - mean_a * mean_a + 1e-05)
    scales_b = lax.rsqrt(square_b / total - mean_b * mean_b + 1e-05)
    unit_a = (values_a - mean_a) * scales_a
    unit_b = (values_b - mean_b) * scales_b
    normed_a = unit_a.astype(jnp.bfloat16)
    normed_b = unit_b.astype(jnp.bfloat16)
    whole_b = lax.all_gather(normed_b, "feat", axis=1, tiled=True)
    partial_value = lax.dot_general(
        normed_a, whole_b, (((0,), (0,)), ((), ())), preferred_element_type=jnp.float32
    )
    row_first = lax.axis_index("feat") * width
    corr = lax.psum(partial_value, "batch") / total
    penalty = penalize(corr, row_first)
    back_a = lax.dot_general(
        whole_b, penalty, (((1,), (1,)), ((), ())), preferred_element_type=jnp.float32
    )
    back_b = lax.psum_scatter(
        lax.dot_general(
            penalty, normed_a, (((0,), (1,)), ((), ())), preferred_element_type=jnp.float32
        ),
        "feat",
        scatter_dimension=0,
        tiled=True,
    ).T
    first_a, second_a, first_b, second_b = lax.psum(
        (
            jnp.sum(back_a, axis=0),
            jnp.sum(back_a * unit_a, axis=0),
            jnp.sum(back_b, axis=0),
            jnp.sum(back_b * unit_b, axis=0),
        ),
        "batch",
    )
    grad_a = backward(back_a, unit_a, scales_a, first_a, second_a, total)
    grad_b = backward(back_b, unit_b, scales_b, first_b, second_b, total)
    return (grad_a, grad_b)


def solution(mesh):
    return jax.shard_map(
        body,
        mesh=mesh,
        in_specs=(P("batch", "feat"), P("batch", "feat")),
        out_specs=(P("batch", "feat"), P("batch", "feat")),
        check_vma=False,
    )
```

profile of v0, /device:TPU:1, one launch (start us, length us, event | category | flops | bytes accessed | tf_op | source)
XLA Modules:
  0.0 450.1 jit_solution(10769003824481131104)
XLA Ops:
  7.2 0.0 all-gather.2.cloned.1.call-start
  7.2 1.3 copy.4
  8.5 0.2 convert_reduce_fusion
  8.7 1.2 fusion
  9.9 13.4 %all-reduce.1 = (f32[512]{0:T(512)S(1)}, f32[512]{0:T(512)S(1)}, f32[512]{0:T(512)S(1)}, f32[512]{0:T(512)S(1)}) all-reduce(f32[512]{0:T(512)S(1)} %get-tuple-element.9, f32[512]{0:T(512)S(1)} %get-tuple-element.8, f32[512]{0:T(512)S(1)} %get-tuple-element.7, f32[512]{0:T(512)S(1)} %get-tuple-element.6), channel_id=1, replica_groups=mesh['batch'=8,'feat'=16] {'batch'}, use_global_device_ids=true, to_apply=%region_7.0 | all-reduce | flops 2048 | bytes 16384 | tf_op jit(solution)/shard_map/psum | solution.py:24
  23.3 1.0 fusion.12
  24.3 0.0 all-gather.2.cloned.1.call-update
  24.4 0.0 all-reduce.4.cloned.1.call-start
  24.4 73.2 %all-gather.2.cloned.1.call-done = bf16[512,8192]{0,1:T(8,128)(2,1)} async-done(((bf16[512,512]{0,1:T(8,128)(2,1)}), bf16[512,8192]{0,1:T(8,128)(2,1)}) %all-gather.2.cloned.1.call-update) | async-done | bytes 8388624 | tf_op jit(solution)/shard_map/all_gather | solution.py:41
  97.6 13.9 %fusion.20 = f32[512,8192]{1,0:T(8,128)} fusion(bf16[512,8192]{0,1:T(8,128)(2,1)} %all-gather.2.cloned.1.call-done, bf16[512,512]{1,0:T(8,128)(2,1)} %param.2, f32[512]{0:T(512)S(1)} %get-tuple-element.19, f32[512]{0:T(512)S(1)} %get-tuple-element.18), kind=kOutput, calls=%fused_computation.28 | convolution fusion | flops 4296015872 | bytes 25694208 | tf_op jit(solution)/shard_map/dot_general | solution.py:42
  111.5 0.0 all-reduce.4.cloned.1.call-update
  111.5 0.0 copy-start.1
  111.5 0.2 reduce-scatter.2.cloned.1.call-start
  111.7 181.7 %all-reduce.4.cloned.1.call-done = f32[512,8192]{1,0:T(8,128)} async-done(((f32[512,8192]{1,0:T(8,128)}), f32[512,8192]{1,0:T(8,128)}) %all-reduce.4.cloned.1.call-update) | async-done | bytes 16777232 | tf_op jit(solution)/shard_map/psum | solution.py:46
  293.4 7.8 %select_convert_fusion = bf16[512,8192]{1,0:T(8,128)(2,1)S(1)} fusion(f32[512,8192]{1,0:T(8,128)} %all-reduce.4.cloned.1.call-done, s32[512]{0:T(512)S(1)} %iota_add_fusion), kind=kLoop, calls=%fused_computation | loop fusion | flops 29360128 | bytes 25167872 | tf_op jit(solution)/shard_map/convert_element_type | solution.py:10
  301.2 0.0 copy-start
  301.2 3.2 copy-done
  304.5 0.0 copy-done.1
  304.5 8.1 %fusion.18 = f32[8192,512]{1,0:T(8,128)} fusion(bf16[512,8192]{1,0:T(8,128)(2,1)S(1)} %select_convert_fusion, bf16[512,512]{1,0:T(8,128)(2,1)S(1)} %copy-done.1, f32[512]{0:T(512)S(1)} %get-tuple-element.19, f32[512]{0:T(512)S(1)} %get-tuple-element.18), kind=kOutput, calls=%fused_computation.27 | convolution fusion | flops 4296015872 | bytes 25694208 | tf_op jit(solution)/shard_map/dot_general | solution.py:52
  312.6 0.0 reduce-scatter.2.cloned.1.call-update
  312.6 9.7 %fusion.22 = (f32[512]{0:T(512)S(1)}, f32[512]{0:T(512)S(1)}, f32[512,512]{1,0:T(8,128)S(1)}) fusion(f32[512]{0:T(512)S(1)} %get-tuple-element.18, f32[512]{0:T(512)S(1)} %get-tuple-element.19, bf16[512,512]{1,0:T(8,128)(2,1)S(1)} %copy-done.1, bf16[512,8192]{0,1:T(8,128)(2,1)} %all-gather.2.cloned.1.call-done, bf16[512,8192]{1,0:T(8,128)(2,1)} %copy-done), kind=kOutput, calls=%fused_computation.38 | convolution fusion | flops 4296539136 | bytes 18358272 | tf_op jit(solution)/shard_map/dot_general | solution.py:48
  322.3 101.6 %reduce-scatter.2.cloned.1.call-done = f32[512,512]{1,0:T(8,128)} async-done(((f32[8192,512]{1,0:T(8,128)}), f32[512,512]{1,0:T(8,128)}) %reduce-scatter.2.cloned.1.call-update) | async-done | bytes 1048592 | tf_op jit(solution)/shard_map/reduce_scatter | solution.py:51
  423.9 1.6 fusion.13
  425.5 1.4 reduce_sum.78
  426.8 13.0 %all-reduce = (f32[512]{0:T(512)S(1)}, f32[512]{0:T(512)S(1)}, f32[512]{0:T(512)S(1)}, f32[512]{0:T(512)S(1)}) all-reduce(f32[512]{0:T(512)S(1)} %get-tuple-element.5, f32[512]{0:T(512)S(1)} %get-tuple-element.4, f32[512]{0:T(512)S(1)} %fusion.13, f32[512]{0:T(512)S(1)} %reduce_sum.78), channel_id=1, replica_groups=mesh['batch'=8,'feat'=16] {'batch'}, use_global_device_ids=true, to_apply=%region_12.13 | all-reduce | flops 2048 | bytes 16384 | tf_op jit(solution)/shard_map/psum | solution.py:59
  439.9 1.6 fusion.16
  441.5 1.0 copy.5
  442.5 1.1 fusion.8
  (5 shorter events, 0.0 us)
Async XLA Ops:
  7.2 90.4 %all-gather.2.cloned.1.call-start = ((), (), s32[]{:S(2)}) async-start(), calls=%async_computation.1 | async-start | bytes 8912896 | tf_op jit(solution)/shard_map/all_gather | solution.py:41
  24.4 269.0 %all-reduce.4.cloned.1.call-start = ((), (), s32[]{:S(2)}) async-start(), calls=%async_computation.2 | async-start | bytes 33554432 | tf_op jit(solution)/shard_map/psum | solution.py:46
  111.5 193.0 %copy-start.1 = (bf16[512,512]{1,0:T(8,128)(2,1)S(1)}, bf16[512,512]{1,0:T(8,128)(2,1)}, u32[]{:S(2)}) copy-start(bf16[512,512]{1,0:T(8,128)(2,1)} %param.2) | copy-start | bytes 1572868
  111.5 312.4 %reduce-scatter.2.cloned.1.call-start = ((), (), s32[]{:S(2)}) async-start(), calls=%async_computation.3 | async-start | bytes 17825792 | tf_op jit(solution)/shard_map/reduce_scatter | solution.py:51
  301.2 3.2 copy-start
Sparse Core Ops, SparseCore 0:
  24.5 73.0 all-gather.1
  111.6 181.7 all-reduce.3
  312.7 111.1 reduce-scatter.1
where the time goes:
time: 452 us; the launch traced here: 450 us
  waiting for transfers between devices  356 us (79%)
  matrix products  31.7 us (7%)
  blocking collectives  26.4 us (6%)
  other arithmetic  15.9 us (4%)
  between operations  13.8 us (3%)
  local copies, waits for them, and re-layouts  5.48 us (1%)
    psum x1, waiting for transfers between devices, body(): corr = lax.psum(partial_value, 'batch') / total  182 us
    reduce_scatter x1, waiting for transfers between devices, body(): lax.psum_scatter(lax.dot_general(penalty, normed_a, (((0,), (1,)), ((), (...  102 us
    all_gather x1, waiting for transfers between devices, body(): whole_b = lax.all_gather(normed_b, 'feat', axis=1, tiled=True)  73.2 us
    dot_general x1, matrix products, body(): lax.dot_general(normed_a, whole_b, (((0,), (0,)), ((), ())), preferred_el...  13.9 us
    psum x1, blocking collectives, body(): lax.psum((jnp.sum(values_a, axis=0), jnp.sum(values_a * values_a, axis=0)...  13.4 us
    psum x1, blocking collectives, body(): lax.psum((jnp.sum(back_a, axis=0), jnp.sum(back_a * unit_a, axis=0), jnp....  13 us
    dot_general x1, matrix products, body(): lax.dot_general(whole_b, penalty, (((1,), (1,)), ((), ())), preferred_ele...  9.7 us
  transfers between devices with their start and end apart: 3, of which 3 were waited for; matrix products, arithmetic and copies ran while one was open for 2% of the time, Pallas kernels for 0%

commit v1 on v0

v1 whole, which is shorter than its diff:
```python
import jax
import jax.numpy as jnp
from jax import lax
from jax.sharding import PartitionSpec as P

LAMBDA = 0.0051


def normalize(whole, total):
    values = whole.astype(jnp.float32)
    mean = jnp.sum(values, axis=0) / total
    square = jnp.sum(values * values, axis=0) / total
    scales = lax.rsqrt(square - mean * mean + 1e-05)
    return mean, scales


def gram(rows, whole):
    partial = lax.dot_general(
        rows, whole, (((1,), (1,)), ((), ())), preferred_element_type=jnp.float32
    ).astype(jnp.bfloat16)
    mine = lax.psum_scatter(partial, "feat", scatter_dimension=1, tiled=True)
    return lax.all_gather(mine, "feat", axis=1, tiled=True)


def backward(back, unit, scales, first_sum, second_sum, total):
    return (scales * (back - first_sum / total - unit * (second_sum / total))).astype(jnp.bfloat16)


def body(view_a, view_b):
    rows_dev, width = view_a.shape
    total = rows_dev * lax.axis_size("batch")
    all_a = lax.all_gather(view_a, "batch", axis=0, tiled=True)
    all_b = lax.all_gather(view_b, "batch", axis=0, tiled=True)
    mean_a, scales_a = normalize(all_a, total)
    mean_b, scales_b = normalize(all_b, total)
    whole_a = ((all_a.astype(jnp.float32) - mean_a) * scales_a).astype(jnp.bfloat16)
    whole_b = ((all_b.astype(jnp.float32) - mean_b) * scales_b).astype(jnp.bfloat16)
    unit_a = (view_a.astype(jnp.float32) - mean_a) * scales_a
    unit_b = (view_b.astype(jnp.float32) - mean_b) * scales_b
    normed_a = unit_a.astype(jnp.bfloat16)
    normed_b = unit_b.astype(jnp.bfloat16)
    gram_b = gram(normed_b, whole_b)
    gram_a = gram(normed_a, whole_a)
    same = jnp.sum(whole_a.astype(jnp.float32) * whole_b.astype(jnp.float32), axis=0) / total
    extra = (2.0 * (same - 1.0)).astype(jnp.bfloat16).astype(jnp.float32) - 2.0 * LAMBDA * same
    factor = 2.0 * LAMBDA / total
    back_a = factor * jnp.dot(
        gram_b, whole_a, preferred_element_type=jnp.float32
    ) + extra * normed_b.astype(jnp.float32)
    back_b = factor * jnp.dot(
        gram_a, whole_b, preferred_element_type=jnp.float32
    ) + extra * normed_a.astype(jnp.float32)
    first_a, second_a, first_b, second_b = lax.psum(
        (
            jnp.sum(back_a, axis=0),
            jnp.sum(back_a * unit_a, axis=0),
            jnp.sum(back_b, axis=0),
            jnp.sum(back_b * unit_b, axis=0),
        ),
        "batch",
    )
    grad_a = backward(back_a, unit_a, scales_a, first_a, second_a, total)
    grad_b = backward(back_b, unit_b, scales_b, first_b, second_b, total)
    return (grad_a, grad_b)


def solution(mesh):
    return jax.shard_map(
        body,
        mesh=mesh,
        in_specs=(P("batch", "feat"), P("batch", "feat")),
        out_specs=(P("batch", "feat"), P("batch", "feat")),
        check_vma=False,
    )
```

time: 452 us -> 387 us (0.86)
  waiting for transfers between devices: 356 us -> 324 us
  blocking collectives: 26.4 us -> 13.5 us
  matrix products: 31.7 us -> 20.9 us
  local copies, waits for them, and re-layouts: 5.48 us -> 0.02 us
    psum x1 -> x0, waiting for transfers between devices: 182 us -> none  [body(): corr = lax.psum(partial_value, 'batch') / total]
    all_gather x1 -> x4, waiting for transfers between devices: 73.2 us -> 171 us  [the longest x2 108 us: gram(): return lax.all_gather(mine, 'feat', axis=1, tiled=True)]
    reduce_scatter x1 -> x2, waiting for transfers between devices: 102 us -> 152 us  [gram(): mine = lax.psum_scatter(partial, 'feat', scatter_dimension=1, tiled=True)]
    psum x1 -> x0, blocking collectives: 13.4 us -> none  [body(): lax.psum((jnp.sum(values_a, axis=0), jnp.sum(values_a * values_a, axis=0)...]
    dot_general x3 -> x4, matrix products: 31.7 us -> 20.9 us  [the longest x2 8.77 us: gram(): lax.dot_general(rows, whole, (((1,), (1,)), ((), ())), preferred_element_...]
    convert_element_type x2 -> x0, other arithmetic: 8.83 us -> none  [the longest x1 7.82 us: penalize(): jnp.where(rows_here == cols_here, 2.0 * (corr - 1.0), 2.0 * 0.0051 * corr)]
    reduce_sum x4 -> x3, other arithmetic: 4.4 us -> 11.5 us  [the longest x2 6.96 us: normalize(): mean = jnp.sum(values, axis=0) / total]
    unnamed x6 -> x8, local copies, waits for them, and re-layouts: 5.48 us -> 0.02 us
  transfers between devices with their start and end apart: 3 -> 6, of which waited for: 3 -> 6; matrix products, arithmetic and copies ran while one was open for 2% -> 7% of each run, Pallas kernels for 0% -> 0%
where the time goes in v1:
time: 387 us; the launch traced here: 386 us
  waiting for transfers between devices  324 us (84%)
  matrix products  20.9 us (5%)
  between operations  14.2 us (4%)
  other arithmetic  13.7 us (4%)
  blocking collectives  13.5 us (3%)
    reduce_scatter x2, waiting for transfers between devices, gram(): mine = lax.psum_scatter(partial, 'feat', scatter_dimension=1, tiled=True)  152 us
    all_gather x2, waiting for transfers between devices, gram(): return lax.all_gather(mine, 'feat', axis=1, tiled=True)  108 us
    all_gather x1, waiting for transfers between devices, body(): all_a = lax.all_gather(view_a, 'batch', axis=0, tiled=True)  36.8 us
    all_gather x1, waiting for transfers between devices, body(): all_b = lax.all_gather(view_b, 'batch', axis=0, tiled=True)  25.8 us
    psum x1, blocking collectives, body(): lax.psum((jnp.sum(back_a, axis=0), jnp.sum(back_a * unit_a, axis=0), jnp....  13.5 us
    dot_general x2, matrix products, gram(): lax.dot_general(rows, whole, (((1,), (1,)), ((), ())), preferred_element_...  8.77 us
  transfers between devices with their start and end apart: 6, of which 6 were waited for; matrix products, arithmetic and copies ran while one was open for 7% of the time, Pallas kernels for 0%

profile of v1, /device:TPU:1, one launch (start us, length us, event | category | flops | bytes accessed | tf_op | source)
XLA Modules:
  0.0 386.2 jit_solution(8912128865778376967)
XLA Ops:
  7.2 0.0 copy-start.2
  7.2 0.0 all-gather.5.cloned.1.call-start
  7.2 0.7 all-gather.5.cloned.1.call-update
  7.9 0.0 all-gather.7.cloned.1.call-start
  8.0 0.7 all-gather.7.cloned.1.call-update
  8.7 0.0 reduce-scatter.5.cloned.1.call-start
  8.7 36.8 %all-gather.5.cloned.1.call-done = bf16[4096,512]{1,0:T(8,128)(2,1)} async-done(((bf16[512,512]{1,0:T(8,128)(2,1)}), bf16[4096,512]{1,0:T(8,128)(2,1)}) %all-gather.5.cloned.1.call-update) | async-done | bytes 4194320 | tf_op jit(solution)/shard_map/all_gather | solution.py:32
  45.5 0.0 copy-start
  45.5 3.5 convert_reduce_fusion.1
  49.0 0.0 copy-done.2
  49.0 0.0 copy-done
  49.0 4.4 %convolution_convert_fusion = bf16[512,4096]{1,0:T(8,128)(2,1)} fusion(bf16[4096,512]{1,0:T(8,128)(2,1)S(1)} %copy-done, f32[512]{0:T(512)S(1)} %get-tuple-element.15, f32[512]{0:T(512)S(1)} %get-tuple-element.14, bf16[512,512]{1,0:T(8,128)(2,1)S(1)} %copy-done.2), kind=kOutput, calls=%fused_computation.13 | convolution fusion | flops 2159017984 | bytes 8916992 | tf_op jit(solution)/shard_map/dot_general | solution.py:18
  53.3 0.0 copy-start.3
  53.4 0.0 reduce-scatter.5.cloned.1.call-update
  53.4 0.0 reduce-scatter.3.cloned.1.call-start
  53.4 25.8 %all-gather.7.cloned.1.call-done = bf16[4096,512]{1,0:T(8,128)(2,1)} async-done(((bf16[512,512]{1,0:T(8,128)(2,1)}), bf16[4096,512]{1,0:T(8,128)(2,1)}) %all-gather.7.cloned.1.call-update) | async-done | bytes 4194320 | tf_op jit(solution)/shard_map/all_gather | solution.py:33
  79.3 0.0 copy-start.1
  79.3 3.5 convert_reduce_fusion
  82.8 0.0 copy-done.3
  82.8 0.0 copy-done.1
  82.8 4.4 %convolution_convert_fusion.1 = bf16[512,4096]{1,0:T(8,128)(2,1)} fusion(bf16[4096,512]{1,0:T(8,128)(2,1)S(1)} %copy-done.1, f32[512]{0:T(512)S(1)} %get-tuple-element.17, f32[512]{0:T(512)S(1)} %get-tuple-element.16, bf16[512,512]{1,0:T(8,128)(2,1)S(1)} %copy-done.3), kind=kOutput, calls=%fused_computation.14 | convolution fusion | flops 2159017984 | bytes 8916992 | tf_op jit(solution)/shard_map/dot_general | solution.py:18
  87.2 0.0 reduce-scatter.3.cloned.1.call-update
  87.2 0.0 all-gather.11.cloned.1.call-start
  87.2 71.1 %reduce-scatter.5.cloned.1.call-done = bf16[512,256]{1,0:T(8,128)(2,1)} async-done(((bf16[512,4096]{1,0:T(8,128)(2,1)}), bf16[512,256]{1,0:T(8,128)(2,1)}) %reduce-scatter.5.cloned.1.call-update) | async-done | bytes 262160 | tf_op jit(solution)/shard_map/reduce_scatter | solution.py:21
  158.4 0.0 all-gather.11.cloned.1.call-update
  158.4 0.2 all-gather.9.cloned.1.call-start
  158.6 80.4 %reduce-scatter.3.cloned.1.call-done = bf16[512,256]{1,0:T(8,128)(2,1)} async-done(((bf16[512,4096]{1,0:T(8,128)(2,1)}), bf16[512,256]{1,0:T(8,128)(2,1)}) %reduce-scatter.3.cloned.1.call-update) | async-done | bytes 262160 | tf_op jit(solution)/shard_map/reduce_scatter | solution.py:21
  239.0 0.0 all-gather.9.cloned.1.call-update
  239.0 4.6 %multiply_reduce_fusion = f32[512]{0:T(512)S(1)} fusion(f32[512]{0:T(512)S(1)} %get-tuple-element.17, f32[512]{0:T(512)S(1)} %get-tuple-element.16, bf16[4096,512]{1,0:T(8,128)(2,1)} %all-gather.7.cloned.1.call-done, f32[512]{0:T(512)S(1)} %get-tuple-element.15, f32[512]{0:T(512)S(1)} %get-tuple-element.14, bf16[4096,512]{1,0:T(8,128)(2,1)} %all-gather.5.cloned.1.call-done), kind=kLoop, calls=%fused_computation.12 | loop fusion | flops 25165312 | bytes 8398848 | tf_op jit(solution)/shard_map/reduce_sum | solution.py:44
  243.6 55.1 %all-gather.11.cloned.1.call-done = bf16[512,4096]{1,0:T(8,128)(2,1)} async-done(((bf16[512,256]{1,0:T(8,128)(2,1)}), bf16[512,4096]{1,0:T(8,128)(2,1)}) %all-gather.11.cloned.1.call-update) | async-done | bytes 4194320 | tf_op jit(solution)/shard_map/all_gather | solution.py:22
  298.7 6.1 %fusion.28 = (f32[512]{0:T(512)S(1)}, f32[512]{0:T(512)S(1)}, f32[512,512]{1,0:T(8,128)S(1)}) fusion(f32[512]{0:T(512)S(1)} %get-tuple-element.17, f32[512]{0:T(512)S(1)} %get-tuple-element.16, bf16[512,512]{1,0:T(8,128)(2,1)S(1)} %copy-done.3, f32[512]{0:T(512)S(1)} %get-tuple-element.15, f32[512]{0:T(512)S(1)} %get-tuple-element.14, ...), kind=kOutput, calls=%fused_computation.39 | convolution fusion | flops 2159541248 | bytes 10500096 | tf_op jit(solution)/shard_map/dot_general | solution.py:50
  304.8 52.9 %all-gather.9.cloned.1.call-done = bf16[512,4096]{1,0:T(8,128)(2,1)} async-done(((bf16[512,256]{1,0:T(8,128)(2,1)}), bf16[512,4096]{1,0:T(8,128)(2,1)}) %all-gather.9.cloned.1.call-update) | async-done | bytes 4194320 | tf_op jit(solution)/shard_map/all_gather | solution.py:22
  357.6 6.1 %fusion.29 = (f32[512]{0:T(512)S(1)}, f32[512]{0:T(512)S(1)}, f32[512,512]{1,0:T(8,128)S(1)}) fusion(f32[512]{0:T(512)S(1)} %get-tuple-element.15, f32[512]{0:T(512)S(1)} %get-tuple-element.14, bf16[512,512]{1,0:T(8,128)(2,1)S(1)} %copy-done.2, f32[512]{0:T(512)S(1)} %get-tuple-element.17, f32[512]{0:T(512)S(1)} %get-tuple-element.16, ...), kind=kOutput, calls=%fused_computation.40 | convolution fusion | flops 2159541248 | bytes 10500096 | tf_op jit(solution)/shard_map/dot_general | solution.py:47
  363.7 13.5 %all-reduce = (f32[512]{0:T(512)S(1)}, f32[512]{0:T(512)S(1)}, f32[512]{0:T(512)S(1)}, f32[512]{0:T(512)S(1)}) all-reduce(f32[512]{0:T(512)S(1)} %get-tuple-element.9, f32[512]{0:T(512)S(1)} %get-tuple-element.8, f32[512]{0:T(512)S(1)} %get-tuple-element.7, f32[512]{0:T(512)S(1)} %get-tuple-element.6), channel_id=1, replica_groups=mesh['batch'=8,'feat'=16] {'batch'}, use_global_device_ids=true, to_apply=%region_9.0 | all-reduce | flops 2048 | bytes 16384 | tf_op jit(solution)/shard_map/psum | solution.py:53
  377.2 1.1 multiply_convert_fusion.1
  378.3 1.1 multiply_convert_fusion
  (5 shorter events, 0.0 us)
Async XLA Ops:
  7.2 41.8 %copy-start.2 = (bf16[512,512]{1,0:T(8,128)(2,1)S(1)}, bf16[512,512]{1,0:T(8,128)(2,1)}, u32[]{:S(2)}) copy-start(bf16[512,512]{1,0:T(8,128)(2,1)} %param.2) | copy-start | bytes 1572868
  7.2 38.3 %all-gather.5.cloned.1.call-start = ((), (), s32[]{:S(2)}) async-start(), calls=%async_computation.2 | async-start | bytes 4718592 | tf_op jit(solution)/shard_map/all_gather | solution.py:32
  7.9 71.3 %all-gather.7.cloned.1.call-start = ((), (), s32[]{:S(2)}) async-start(), calls=%async_computation.3 | async-start | bytes 4718592 | tf_op jit(solution)/shard_map/all_gather | solution.py:33
  8.7 149.7 %reduce-scatter.5.cloned.1.call-start = ((), (), s32[]{:S(2)}) async-start(), calls=%async_computation.6 | async-start | bytes 4456448 | tf_op jit(solution)/shard_map/reduce_scatter | solution.py:21
  45.5 3.5 copy-start
  53.3 29.4 %copy-start.3 = (bf16[512,512]{1,0:T(8,128)(2,1)S(1)}, bf16[512,512]{1,0:T(8,128)(2,1)}, u32[]{:S(2)}) copy-start(bf16[512,512]{1,0:T(8,128)(2,1)} %param.3) | copy-start | bytes 1572868
  53.4 185.6 %reduce-scatter.3.cloned.1.call-start = ((), (), s32[]{:S(2)}) async-start(), calls=%async_computation.4 | async-start | bytes 4456448 | tf_op jit(solution)/shard_map/reduce_scatter | solution.py:21
  79.3 3.5 copy-start.1
  87.2 211.5 %all-gather.11.cloned.1.call-start = ((), (), s32[]{:S(2)}) async-start(), calls=%async_computation.7 | async-start | bytes 4456448 | tf_op jit(solution)/shard_map/all_gather | solution.py:22
  158.4 199.3 %all-gather.9.cloned.1.call-start = ((), (), s32[]{:S(2)}) async-start(), calls=%async_computation.5 | async-start | bytes 4456448 | tf_op jit(solution)/shard_map/all_gather | solution.py:22
Sparse Core Ops, SparseCore 0:
  9.7 35.6 all-gather.4
  47.2 32.0 all-gather.6
  82.6 75.7 reduce-scatter.4
  161.9 77.0 reduce-scatter.2
  240.9 57.6 all-gather.10
  300.7 56.9 all-gather.8

commit v2 on v1

v2 whole, which is shorter than its diff:
```python
import functools

import jax
import jax.numpy as jnp
from jax import lax
from jax.experimental import pallas as pl
from jax.experimental.pallas import tpu as pltpu
from jax.sharding import PartitionSpec as P

LAMBDA = 0.0051
MESH = pl.DeviceIdType.MESH
F32 = jnp.float32
BF16 = jnp.bfloat16
COPIES = 256
REDUCED = (1024, 1024, 512)
GATHERED = (1024, 2048, 1024)


def rem4(value):
    return lax.rem(value, 4)


class Net:
    def __init__(self, send_sems, recv_sems):
        self.send_sems, self.recv_sems, self.copies = send_sems, recv_sems, []

    def copy(self, src, dst, device):
        n = len(self.copies)
        item = pltpu.make_async_remote_copy(
            src_ref=src,
            dst_ref=dst,
            send_sem=self.send_sems.at[n],
            recv_sem=self.recv_sems.at[n],
            device_id=device,
            device_id_type=MESH,
        )
        item.start()
        self.copies.append(item)
        return item

    def finish(self):
        for item in self.copies:
            item.wait_send()


def kernel(rows, total, va, vb, ga, gb, *scratch):
    (raw, normed, stat, same, last_a, last_b, moments, acc, send_sems, recv_sems) = scratch[:10]
    blocks = scratch[10:]
    net = Net(send_sems, recv_sems)
    views = (va, vb)
    batch, feat = lax.axis_index("batch"), lax.axis_index("feat")
    x, core = batch // 2, lax.rem(batch, 2)
    y, z = feat // 4, rem4(feat)

    def at_batch(dx, dcore):
        return (rem4(x + dx) * 2 + lax.rem(core + dcore, 2), feat)

    def at_feat(half, d1, d2):
        dy, dz = (d1, d2) if half == 0 else (d2, d1)
        return (batch, rem4(y + dy) * 4 + rem4(z + dz))

    peers = [(lax.rem(batch + k, 8), feat) for k in range(1, 8)]
    planes = [at_feat(half, k, 0) for half in range(2) for k in range(1, 4)]
    barrier = pltpu.get_barrier_semaphore()
    for device in peers + planes:
        pl.semaphore_signal(barrier, inc=1, device_id=device, device_id_type=MESH)

    def sums(step, carry):
        out = []
        for v in range(2):
            values = views[v][pl.ds(pl.multiple_of(step * 64, 64), 64), :].astype(F32)
            out.append(carry[2 * v] + jnp.sum(values.reshape(8, 8, -1), axis=0))
            out.append(carry[2 * v + 1] + jnp.sum((values * values).reshape(8, 8, -1), axis=0))
        return tuple(out)

    zero = jnp.zeros((8, rows), F32)
    parts = lax.fori_loop(0, rows // 64, sums, (zero,) * 4)
    for k in range(4):
        stat[batch, pl.ds(k, 1), :] = jnp.sum(parts[k], axis=0, keepdims=True)
    stat[batch, pl.ds(4, 4), :] = jnp.zeros((4, rows), F32)

    pl.semaphore_wait(barrier, len(peers) + len(planes))

    def exchange(ref):
        return [net.copy(ref.at[batch], ref.at[batch], device) for device in peers]

    def collect(ref, items):
        for item in items:
            item.wait_recv()
        result = ref[0]
        for k in range(1, 8):
            result = result + ref[k]
        return result

    stat_items = exchange(stat)
    sibling = (batch + 1 - 2 * core, feat)
    to_sib = {}
    near = {}
    far = {}
    for v in (1, 0):
        to_sib[v, 0] = net.copy(views[v], raw.at[v, 1], sibling)
        if v == 1:
            near[v] = (
                net.copy(views[v], raw.at[v, 6], at_batch(1, 0)),
                net.copy(views[v], raw.at[v, 2], at_batch(3, 0)),
            )

    sum_all = collect(stat, stat_items)
    for v in range(2):
        mean = sum_all[2 * v : 2 * v + 1] / total
        square = sum_all[2 * v + 1 : 2 * v + 2] / total
        moments[pl.ds(2 * v, 1), :] = mean
        moments[pl.ds(2 * v + 1, 1), :] = lax.rsqrt(square - mean * mean + 1e-05)

    def normalize(v, slot):
        source = views[v] if slot == 0 else raw.at[v, slot]

        @pl.loop(0, rows // 64)
        def _(step):
            here = pl.ds(pl.multiple_of(step * 64, 64), 64)
            values = source[here, :].astype(F32)
            unit = (values - moments[pl.ds(2 * v, 1), :]) * moments[pl.ds(2 * v + 1, 1), :]
            normed[v, slot, here, :] = unit.astype(BF16)

    def own_rows(v):
        normalize(v, 0)
        to_sib[v, 0].wait_recv()
        normalize(v, 1)

    def near_rows(v):
        from_left, from_right = near[v]
        from_left.wait_recv()
        from_right.wait_recv()
        half = rows // 2
        first, second = pl.ds(0, half), pl.ds(half, half)
        far[v] = (
            net.copy(raw.at[v, 6, first], raw.at[v, 4, first], at_batch(1, 0)),
            net.copy(raw.at[v, 2, second], raw.at[v, 4, second], at_batch(3, 0)),
        )
        to_sib[v, 2] = net.copy(raw.at[v, 2], raw.at[v, 3], sibling)
        to_sib[v, 6] = net.copy(raw.at[v, 6], raw.at[v, 7], sibling)
        if v == 1:
            near[0] = (
                net.copy(views[0], raw.at[0, 6], at_batch(1, 0)),
                net.copy(views[0], raw.at[0, 2], at_batch(3, 0)),
            )
        normalize(v, 2)
        normalize(v, 6)
        for slot in (2, 6):
            to_sib[v, slot].wait_recv()
            normalize(v, slot + 1)

    def far_rows(v):
        for item in far[v]:
            item.wait_recv()
        to_sib[v, 4] = net.copy(raw.at[v, 4], raw.at[v, 5], sibling)
        normalize(v, 4)
        to_sib[v, 4].wait_recv()
        normalize(v, 5)

    turned = x // 2

    class Block:
        def __init__(self, v, kind):
            self.v, self.kind = v, kind
            base = (v * 3 + kind) * 7
            (self.part, self.r1r, self.r1l, self.r2r, self.r2l, self.r3, self.full) = blocks[
                base : base + 7
            ]
            self.columns = REDUCED[kind]

        def mine(self, half):
            return (y, z) if half == 0 else (z, y)

        def product(self):
            v = self.v
            if self.kind == 0:
                own_rows(v)
            elif self.kind == 1:
                near_rows(v)
            else:
                far_rows(v)

            @pl.loop(0, rows // 128)
            def _(step):
                left = normed[v, 0, pl.ds(pl.multiple_of(step * 128, 128), 128), :]
                if self.kind == 2:
                    right = normed[v, 4 + turned]
                else:
                    right = normed[v, pl.ds(2 * self.kind, 2)].reshape(2 * rows, rows)
                value = lax.dot_general(
                    left, right, (((1,), (1,)), ((), ())), preferred_element_type=F32
                )
                self.part[pl.ds(step * 8, 8)] = value.astype(BF16).reshape(8, 16, self.columns)

            self.one = []
            for half in range(2):
                m1, _ = self.mine(half)
                base = half * 16 + rem4(m1 + 2) * 4
                self.one.append(
                    (
                        net.copy(
                            self.part.at[pl.ds(base + 2, 2)],
                            self.r1r.at[half],
                            at_feat(half, 1, 0),
                        ),
                        net.copy(
                            self.part.at[pl.ds(base, 2)], self.r1l.at[half], at_feat(half, 3, 0)
                        ),
                    )
                )

        def pass_on(self):
            self.two = []
            for half in range(2):
                m1, _ = self.mine(half)
                right = half * 16 + rem4(m1 + 1) * 4
                left = half * 16 + rem4(m1 + 3) * 4
                from_left, from_right = self.one[half]
                from_left.wait_recv()
                here = pl.ds(right + 2, 2)
                self.part[here] = (
                    self.part[here].astype(F32) + self.r1r[half].astype(F32)
                ).astype(BF16)
                first = net.copy(
                    self.part.at[pl.ds(right, 4)], self.r2r.at[half], at_feat(half, 1, 0)
                )
                from_right.wait_recv()
                here = pl.ds(left, 2)
                self.part[here] = (
                    self.part[here].astype(F32) + self.r1l[half].astype(F32)
                ).astype(BF16)
                second = net.copy(
                    self.part.at[pl.ds(left, 4)], self.r2l.at[half], at_feat(half, 3, 0)
                )
                self.two.append((first, second))

        def turn(self):
            self.three = []
            for half in range(2):
                m1, m2 = self.mine(half)
                base = half * 16 + m1 * 4
                for item in self.two[half]:
                    item.wait_recv()
                here = pl.ds(base, 4)
                self.part[here] = (
                    self.part[here].astype(F32)
                    + self.r2r[half].astype(F32)
                    + self.r2l[half].astype(F32)
                ).astype(BF16)
                self.three.append(
                    [
                        net.copy(
                            self.part.at[base + rem4(m2 + k)],
                            self.r3.at[half, k - 1],
                            at_feat(half, 0, k),
                        )
                        for k in range(1, 4)
                    ]
                )

        def own(self, half):
            m1, m2 = self.mine(half)
            return half * 16 + m1 * 4 + m2

        def reduced(self):
            self.mirror = []
            for half in range(2):
                for item in self.three[half]:
                    item.wait_recv()
                own = self.own(half)
                value = self.part[own].astype(F32)
                for k in range(3):
                    value = value + self.r3[half, k].astype(F32)
                self.full[own, :, pl.ds(0, self.columns)] = value.astype(BF16)
                if self.kind == 1:
                    for k in range(2):
                        self.mirror.append(
                            net.copy(
                                self.full.at[own, :, pl.ds(512 * k, 512)],
                                self.full.at[own, :, pl.ds(1024 + 512 * k, 512)],
                                at_batch(1, k),
                            )
                        )
                if self.kind == 2:
                    self.mirror.append(
                        net.copy(
                            self.full.at[own, :, pl.ds(0, 512)],
                            self.full.at[own, :, pl.ds(512, 512)],
                            at_batch(2, turned),
                        )
                    )
            if self.kind == 0:
                self.spread()

        def spread(self):
            for item in self.mirror:
                item.wait_recv()
            self.four = []
            for half in range(2):
                own = self.own(half)
                self.four.append(
                    [
                        net.copy(self.full.at[own], self.full.at[own], at_feat(half, 0, k))
                        for k in range(1, 4)
                    ]
                )

        def gather(self):
            self.five = []
            for half in range(2):
                m1, _ = self.mine(half)
                for item in self.four[half]:
                    item.wait_recv()
                here = self.full.at[pl.ds(half * 16 + m1 * 4, 4)]
                self.five.append(
                    (
                        net.copy(here, here, at_feat(half, 1, 0)),
                        net.copy(here, here, at_feat(half, 3, 0)),
                    )
                )

        def gather_on(self):
            self.six = []
            for half in range(2):
                m1, _ = self.mine(half)
                from_left, from_right = self.five[half]
                from_left.wait_recv()
                here = self.full.at[pl.ds(half * 16 + rem4(m1 + 3) * 4, 2)]
                first = net.copy(here, here, at_feat(half, 1, 0))
                from_right.wait_recv()
                here = self.full.at[pl.ds(half * 16 + rem4(m1 + 1) * 4 + 2, 2)]
                second = net.copy(here, here, at_feat(half, 3, 0))
                self.six.append((first, second))

        def apply(self):
            for half in range(2):
                for item in self.six[half]:
                    item.wait_recv()
            v, other = self.v, 1 - self.v

            @pl.loop(0, rows // 128)
            def _(step):
                here = pl.ds(pl.multiple_of(step * 128, 128), 128)
                left = self.full[pl.ds(step * 8, 8), :, pl.ds(0, self.columns)].reshape(
                    128, self.columns
                )
                if self.kind == 2:
                    right = normed[other, 4 + turned]
                else:
                    right = normed[other, pl.ds(2 * self.kind, 2)].reshape(2 * rows, rows)
                value = jnp.dot(left, right, preferred_element_type=F32)
                for k in range(GATHERED[self.kind] // 512 - self.columns // 512):
                    start = pl.multiple_of(self.columns + 512 * k + step * 128, 128)
                    left = self.full[:, :, pl.ds(start, 128)].reshape(rows, 128)
                    slot = 6 + k if self.kind == 1 else 5 - turned
                    value = value + lax.dot_general(
                        left,
                        normed[other, slot],
                        (((0,), (0,)), ((), ())),
                        preferred_element_type=F32,
                    )
                if self.kind == 0:
                    acc[other, here, :] = value
                else:
                    acc[other, here, :] = acc[other, here, :] + value

        def stages(self):
            steps = [self.product, self.pass_on, self.turn, self.reduced]
            if self.kind != 0:
                steps.append(self.spread)
            return steps + [self.gather, self.gather_on, self.apply]

    same_items = []

    def diagonal():
        def step_sum(step, carry):
            here = pl.ds(pl.multiple_of(step * 64, 64), 64)
            both = normed[0, 0, here, :].astype(F32) * normed[1, 0, here, :].astype(F32)
            return carry + jnp.sum(both.reshape(8, 8, -1), axis=0)

        part = lax.fori_loop(0, rows // 64, step_sum, zero)
        same[batch] = part
        same_items.extend(exchange(same))

    start = {(1, 0): 0, (0, 0): 1, (1, 1): 2, (1, 2): 3, (0, 1): 5, (0, 2): 6}
    running = [(begin, Block(v, kind)) for (v, kind), begin in start.items()]
    for tick in range(16):
        for begin, block in running:
            steps = block.stages()
            if 0 <= tick - begin < len(steps):
                steps[tick - begin]()
        if tick == 1:
            diagonal()

    cosine = jnp.sum(collect(same, same_items), axis=0, keepdims=True) / total
    extra = (2.0 * (cosine - 1.0)).astype(BF16).astype(F32) - 2.0 * LAMBDA * cosine
    factor = 2.0 * LAMBDA / total

    def unit_of(v, here):
        values = views[v][here, :].astype(F32)
        return (values - moments[pl.ds(2 * v, 1), :]) * moments[pl.ds(2 * v + 1, 1), :]

    def back_sums(v, last):
        def step_sum(step, carry):
            here = pl.ds(pl.multiple_of(step * 64, 64), 64)
            back = factor * acc[v, here, :] + extra * normed[1 - v, 0, here, :].astype(F32)
            acc[v, here, :] = back
            first = carry[0] + jnp.sum(back.reshape(8, 8, -1), axis=0)
            second = carry[1] + jnp.sum((back * unit_of(v, here)).reshape(8, 8, -1), axis=0)
            return first, second

        first, second = lax.fori_loop(0, rows // 64, step_sum, (zero, zero))
        last[batch, pl.ds(0, 1), :] = jnp.sum(first, axis=0, keepdims=True)
        last[batch, pl.ds(1, 1), :] = jnp.sum(second, axis=0, keepdims=True)
        last[batch, pl.ds(2, 6), :] = jnp.zeros((6, rows), F32)
        return exchange(last)

    def finish(v, last, items, out):
        both = collect(last, items) / total
        first, second = both[0:1], both[1:2]

        @pl.loop(0, rows // 64)
        def _(step):
            here = pl.ds(pl.multiple_of(step * 64, 64), 64)
            scale = moments[pl.ds(2 * v + 1, 1), :]
            value = scale * (acc[v, here, :] - first - unit_of(v, here) * second)
            out[here, :] = value.astype(BF16)

    items_a = back_sums(0, last_a)
    items_b = back_sums(1, last_b)
    finish(0, last_a, items_a, ga)
    finish(1, last_b, items_b, gb)
    net.finish()


def body(view_a, view_b):
    rows, width = view_a.shape
    total = rows * lax.axis_size("batch")
    blocks = []
    for _ in range(2):
        for columns, wide in zip(REDUCED, GATHERED):
            blocks += [
                pltpu.VMEM((32, 16, columns), BF16),
                pltpu.VMEM((2, 2, 16, columns), BF16),
                pltpu.VMEM((2, 2, 16, columns), BF16),
                pltpu.VMEM((2, 4, 16, columns), BF16),
                pltpu.VMEM((2, 4, 16, columns), BF16),
                pltpu.VMEM((2, 3, 16, columns), BF16),
                pltpu.VMEM((32, 16, wide), BF16),
            ]
    vmem = pl.BlockSpec(memory_space=pltpu.VMEM)
    return pl.pallas_call(
        functools.partial(kernel, rows, total),
        out_shape=(jax.ShapeDtypeStruct((rows, width), BF16),) * 2,
        in_specs=[vmem, vmem],
        out_specs=(vmem, vmem),
        scratch_shapes=[
            pltpu.VMEM((2, 8, rows, width), BF16),
            pltpu.VMEM((2, 8, rows, width), BF16),
            pltpu.VMEM((8, 8, width), F32),
            pltpu.VMEM((8, 8, width), F32),
            pltpu.VMEM((8, 8, width), F32),
            pltpu.VMEM((8, 8, width), F32),
            pltpu.VMEM((8, width), F32),
            pltpu.VMEM((2, rows, width), F32),
            pltpu.SemaphoreType.DMA((COPIES,)),
            pltpu.SemaphoreType.DMA((COPIES,)),
        ]
        + blocks,
        compiler_params=pltpu.CompilerParams(
            collective_id=0, has_side_effects=True, vmem_limit_bytes=56 * 2**20
        ),
        name="gram_gradient",
    )(view_a, view_b)


def solution(mesh):
    return jax.shard_map(
        body,
        mesh=mesh,
        in_specs=(P("batch", "feat"), P("batch", "feat")),
        out_specs=(P("batch", "feat"), P("batch", "feat")),
        check_vma=False,
    )
```

time: 387 us -> 124 us (0.32)
  waiting for transfers between devices: 324 us -> 0 us
  Pallas kernels: 0 us -> 120 us
  matrix products: 20.9 us -> 0 us
  other arithmetic: 13.7 us -> 0 us
  between operations: 14.2 us -> 0.65 us
  blocking collectives: 13.5 us -> 0 us
    all_gather x4 -> x0, waiting for transfers between devices: 171 us -> none  [the longest x2 108 us: gram(): return lax.all_gather(mine, 'feat', axis=1, tiled=True)]
    reduce_scatter x2 -> x0, waiting for transfers between devices: 152 us -> none  [gram(): mine = lax.psum_scatter(partial, 'feat', scatter_dimension=1, tiled=True)]
    pallas_call x0 -> x1, Pallas kernels: none -> 120 us  [body(): pl.pallas_call(functools.partial(kernel, rows, total), out_shape=(jax.Sha...]
    dot_general x4 -> x0, matrix products: 20.9 us -> none  [the longest x2 8.77 us: gram(): lax.dot_general(rows, whole, (((1,), (1,)), ((), ())), preferred_element_...]
    psum x1 -> x0, blocking collectives: 13.5 us -> none  [body(): lax.psum((jnp.sum(back_a, axis=0), jnp.sum(back_a * unit_a, axis=0), jnp....]
    reduce_sum x3 -> x0, other arithmetic: 11.5 us -> none  [the longest x2 6.96 us: normalize(): mean = jnp.sum(values, axis=0) / total]
  transfers between devices with their start and end apart: 6 -> 0, of which waited for: 6 -> 0; matrix products, arithmetic and copies ran while one was open for 7% -> 0% of each run, Pallas kernels for 0% -> 0%
where the time goes in v2:
time: 124 us; the launch traced here: 123 us
  Pallas kernels  120 us (97%)
  local copies, waits for them, and re-layouts  2.72 us (2%)
    pallas_call x1, Pallas kernels, body(): pl.pallas_call(functools.partial(kernel, rows, total), out_shape=(jax.Sha...  120 us
    unnamed x4, local copies, waits for them, and re-layouts  2.72 us

profile of v2, /device:TPU:1, one launch (start us, length us, event | category | flops | bytes accessed | tf_op | source)
XLA Modules:
  0.0 123.5 jit_solution(1475612574199868217)
XLA Ops:
  0.6 120.1 %gram_gradient.1 = (bf16[512,512]{1,0:T(8,128)(2,1)}, bf16[512,512]{1,0:T(8,128)(2,1)}) custom-call(bf16[512,512]{1,0:T(8,128)(2,1)} %va.1, bf16[512,512]{1,0:T(8,128)(2,1)} %vb.1), custom_call_target="tpu_custom_call" | custom-call | tf_op jit(solution)/shard_map/gram_gradient/pallas_call | solution.py:453
  120.7 0.0 copy-start
  120.7 1.9 %copy.6 = bf16[512,512]{1,0:T(8,128)(2,1)} copy(bf16[512,512]{1,0:T(8,128)(2,1)} %get-tuple-element.4) | data formatting | bytes 1048576
  122.7 0.0 copy-done
  122.7 0.8 copy.7
Async XLA Ops:
  120.7 1.9 %copy-start = (bf16[512,512]{1,0:T(8,128)(2,1)S(1)}, bf16[512,512]{1,0:T(8,128)(2,1)}, u32[]{:S(2)}) copy-start(bf16[512,512]{1,0:T(8,128)(2,1)} %get-tuple-element.5) | copy-start | bytes 1572868

commit v3 on v2

v3 whole, which is shorter than its diff:
```python
import functools

import jax
import jax.numpy as jnp
from jax import lax
from jax.experimental import pallas as pl
from jax.experimental.pallas import tpu as pltpu
from jax.sharding import PartitionSpec as P

LAMBDA = 0.0051
MESH = pl.DeviceIdType.MESH
F32 = jnp.float32
BF16 = jnp.bfloat16
SENDS, RECEIVES = 20, 60
REDUCED = (768, 1024, 512)
GATHERED = (768, 2048, 1024)


def rem4(value):
    return lax.rem(value, 4)


class Net:
    def __init__(self, send_sems, recv_sems):
        self.send_sems, self.recv_sems = send_sems, recv_sems
        self.sends, self.receives = [], 0

    def sender(self, moved):
        self.sends.append(moved)
        return self.send_sems.at[len(self.sends) - 1]

    def receiver(self):
        self.receives += 1
        return self.recv_sems.at[self.receives - 1]

    def finish(self):
        for n, moved in enumerate(self.sends):
            wait(self.send_sems.at[n], moved)


def send(src, dst, sender, receiver, device):
    pltpu.make_async_remote_copy(
        src_ref=src,
        dst_ref=dst,
        send_sem=sender,
        recv_sem=receiver,
        device_id=device,
        device_id_type=MESH,
    ).start()


def wait(sem, moved):
    pltpu.make_async_copy(moved, moved, sem).wait()


def kernel(rows, total, va, vb, ga, gb, *scratch):
    (raw, normed, stat, same, last_a, last_b, moments, acc, cross, send_sems, recv_sems) = scratch[:11]
    blocks = scratch[11:]
    net = Net(send_sems, recv_sems)
    views = (va, vb)
    batch, feat = lax.axis_index("batch"), lax.axis_index("feat")
    x, core = batch // 2, lax.rem(batch, 2)
    y, z = feat // 4, rem4(feat)

    def at_batch(dx, dcore):
        return (rem4(x + dx) * 2 + lax.rem(core + dcore, 2), feat)

    def at_feat(half, d1, d2):
        dy, dz = (d1, d2) if half == 0 else (d2, d1)
        return (batch, rem4(y + dy) * 4 + rem4(z + dz))

    peers = [(lax.rem(batch + k, 8), feat) for k in range(1, 8)]
    planes = [at_feat(half, k, 0) for half in range(2) for k in range(1, 4)]
    barrier = pltpu.get_barrier_semaphore()
    for device in peers + planes:
        pl.semaphore_signal(barrier, inc=1, device_id=device, device_id_type=MESH)

    def sums(step, carry):
        out = []
        for v in range(2):
            values = views[v][pl.ds(pl.multiple_of(step * 64, 64), 64), :].astype(F32)
            out.append(carry[2 * v] + jnp.sum(values.reshape(8, 8, -1), axis=0))
            out.append(carry[2 * v + 1] + jnp.sum((values * values).reshape(8, 8, -1), axis=0))
        return tuple(out)

    zero = jnp.zeros((8, rows), F32)
    parts = lax.fori_loop(0, rows // 64, sums, (zero,) * 4)
    for k in range(4):
        stat[batch, pl.ds(k, 1), :] = jnp.sum(parts[k], axis=0, keepdims=True)
    stat[batch, pl.ds(4, 4), :] = jnp.zeros((4, rows), F32)

    pl.semaphore_wait(barrier, len(peers) + len(planes))

    def exchange(ref):
        sender, receiver = net.sender(ref.at[pl.ds(0, 7)]), net.receiver()
        for device in peers:
            send(ref.at[batch], ref.at[batch], sender, receiver, device)
        return receiver

    def collect(ref, receiver):
        wait(receiver, ref.at[pl.ds(0, 7)])
        result = ref[0]
        for k in range(1, 8):
            result = result + ref[k]
        return result

    stat_items = exchange(stat)
    sibling = (batch + 1 - 2 * core, feat)
    half = rows // 2
    upper, lower = pl.ds(0, half), pl.ds(half, half)
    view_sends = [net.sender(raw.at[v, pl.ds(0, 7)]) for v in range(2)]
    view_sems = [[net.receiver() for _ in range(7)] for _ in range(2)]

    def send_rows(v, src, slot, device, part=None):
        dst = raw.at[v, slot] if part is None else raw.at[v, slot, part]
        send(src, dst, view_sends[v], view_sems[v][slot - 1], device)

    def wait_rows(v, slot):
        wait(view_sems[v][slot - 1], raw.at[v, slot])

    def send_near(v):
        send_rows(v, views[v], 6, at_batch(1, 0))
        send_rows(v, views[v], 2, at_batch(3, 0))

    send_near(1)
    for v in (1, 0):
        send_rows(v, views[v], 1, sibling)

    sum_all = collect(stat, stat_items)
    for v in range(2):
        mean = sum_all[2 * v : 2 * v + 1] / total
        square = sum_all[2 * v + 1 : 2 * v + 2] / total
        moments[pl.ds(2 * v, 1), :] = mean
        moments[pl.ds(2 * v + 1, 1), :] = lax.rsqrt(square - mean * mean + 1e-05)

    def normalize(v, slot):
        source = views[v] if slot == 0 else raw.at[v, slot]

        @pl.loop(0, rows // 64)
        def _(step):
            here = pl.ds(pl.multiple_of(step * 64, 64), 64)
            values = source[here, :].astype(F32)
            unit = (values - moments[pl.ds(2 * v, 1), :]) * moments[pl.ds(2 * v + 1, 1), :]
            normed[v, slot, here, :] = unit.astype(BF16)

    def own_rows(v):
        normalize(v, 0)
        wait_rows(v, 1)
        normalize(v, 1)

    def near_rows(v):
        wait_rows(v, 6)
        wait_rows(v, 2)
        send_rows(v, raw.at[v, 6, upper], 4, at_batch(1, 0), upper)
        send_rows(v, raw.at[v, 2, lower], 4, at_batch(3, 0), lower)
        send_rows(v, raw.at[v, 2], 3, sibling)
        send_rows(v, raw.at[v, 6], 7, sibling)
        if v == 1:
            send_near(0)
        normalize(v, 2)
        normalize(v, 6)
        for slot in (3, 7):
            wait_rows(v, slot)
            normalize(v, slot)

    def far_rows(v):
        wait_rows(v, 4)
        send_rows(v, raw.at[v, 4], 5, sibling)
        normalize(v, 4)
        wait_rows(v, 5)
        normalize(v, 5)

    net.cross_sends = [net.sender(cross.at[v]) for v in range(2)]

    def cross_rows(part, turn):
        return pl.ds(pl.multiple_of(lax.rem(part + turn, 2) * 256, 256), 256)

    turned = x // 2

    class Block:
        def __init__(self, v, kind):
            self.v, self.kind = v, kind
            base = (v * 3 + kind) * 5
            self.part, self.r1, self.r2, self.r3, self.full = blocks[base : base + 5]
            self.cross = cross.at[v]
            self.columns = REDUCED[kind]
            mirrored = 0 if kind == 0 else 1
            self.reduce_send = net.sender(self.part.at[pl.ds(0, 30)])
            self.gather_send = net.sender(self.full.at[pl.ds(0, 30 + mirrored)])
            self.sems = [net.receiver() for _ in range(7)]

        def mine(self, half):
            return (y, z) if half == 0 else (z, y)

        def product(self):
            v = self.v
            if self.kind == 0:
                own_rows(v)
            elif self.kind == 1:
                near_rows(v)
            else:
                far_rows(v)

            @pl.loop(0, rows // 128)
            def _(step):
                left = normed[v, 0, pl.ds(pl.multiple_of(step * 128, 128), 128), :]

                def block(first, right):
                    value = lax.dot_general(
                        left, right, (((1,), (1,)), ((), ())), preferred_element_type=F32
                    )
                    width = right.shape[0]
                    self.part[pl.ds(step * 8, 8), :, pl.ds(first, width)] = value.astype(
                        BF16
                    ).reshape(8, 16, width)

                if self.kind == 0:
                    block(0, normed[v, 0])
                    block(rows, normed[v, 1, cross_rows(step // 2, core), :])
                elif self.kind == 1:
                    block(0, normed[v, pl.ds(2, 2)].reshape(2 * rows, rows))
                else:
                    block(0, normed[v, 4 + turned])

            for half in range(2):
                m1, _ = self.mine(half)
                base = half * 16 + rem4(m1 + 2) * 4
                for k in range(2):
                    send(
                        self.part.at[pl.ds(base + 2 * (1 - k), 2)],
                        self.r1.at[half, k],
                        self.reduce_send,
                        self.sems[0],
                        at_feat(half, 1 + 2 * k, 0),
                    )

        def pass_on(self):
            wait(self.sems[0], self.r1)
            for half in range(2):
                m1, _ = self.mine(half)
                for k in range(2):
                    base = half * 16 + rem4(m1 + 1 + 2 * k) * 4
                    here = pl.ds(base + 2 * (1 - k), 2)
                    self.part[here] = (
                        self.part[here].astype(F32) + self.r1[half, k].astype(F32)
                    ).astype(BF16)
                    send(
                        self.part.at[pl.ds(base, 4)],
                        self.r2.at[half, k],
                        self.reduce_send,
                        self.sems[1],
                        at_feat(half, 1 + 2 * k, 0),
                    )

        def turn(self):
            wait(self.sems[1], self.r2)
            for half in range(2):
                m1, m2 = self.mine(half)
                base = half * 16 + m1 * 4
                here = pl.ds(base, 4)
                self.part[here] = (
                    self.part[here].astype(F32)
                    + self.r2[half, 0].astype(F32)
                    + self.r2[half, 1].astype(F32)
                ).astype(BF16)
                for k in range(1, 4):
                    send(
                        self.part.at[base + rem4(m2 + k)],
                        self.r3.at[half, k - 1],
                        self.reduce_send,
                        self.sems[2],
                        at_feat(half, 0, k),
                    )

        def own(self, half):
            m1, m2 = self.mine(half)
            return half * 16 + m1 * 4 + m2

        def mirror(self, own, first, start, device):
            send(
                self.full.at[own, :, pl.ds(first, 512)],
                self.full.at[own, :, pl.ds(start, 512)],
                self.gather_send,
                self.sems[3],
                device,
            )

        def reduced(self):
            wait(self.sems[2], self.r3)
            for half in range(2):
                own = self.own(half)
                value = self.part[own].astype(F32)
                for k in range(3):
                    value = value + self.r3[half, k].astype(F32)
                self.full[own, :, pl.ds(0, self.columns)] = value.astype(BF16)
                if self.kind == 1:
                    for k in range(2):
                        self.mirror(own, 512 * k, 1024 + 512 * k, at_batch(1, k))
                if self.kind == 2:
                    self.mirror(own, 0, 512, at_batch(2, turned))
            if self.kind == 0:
                self.spread()

        def spread(self):
            if self.kind != 0:
                wait(self.sems[3], self.full.at[pl.ds(0, 1)])
            for half in range(2):
                here = self.full.at[self.own(half)]
                for k in range(1, 4):
                    send(here, here, self.gather_send, self.sems[4], at_feat(half, 0, k))

        def gather(self):
            wait(self.sems[4], self.full.at[pl.ds(0, 6)])
            for half in range(2):
                m1, _ = self.mine(half)
                here = self.full.at[pl.ds(half * 16 + m1 * 4, 4)]
                for k in range(2):
                    send(here, here, self.gather_send, self.sems[5], at_feat(half, 1 + 2 * k, 0))

        def gather_on(self):
            wait(self.sems[5], self.full.at[pl.ds(0, 16)])
            for half in range(2):
                m1, _ = self.mine(half)
                for k in range(2):
                    base = half * 16 + rem4(m1 + 3 + 2 * k) * 4
                    here = self.full.at[pl.ds(base + 2 * k, 2)]
                    send(here, here, self.gather_send, self.sems[6], at_feat(half, 1 + 2 * k, 0))

        def arrived(self):
            wait(self.sems[6], self.full.at[pl.ds(0, 8)])

        def swap(self):
            self.arrived()
            send(
                self.full.at[:, :, pl.ds(rows, rows // 2)],
                self.cross,
                net.cross_sends[self.v],
                self.sems[3],
                sibling,
            )

        def apply(self):
            if self.kind == 0:
                wait(self.sems[3], self.cross)
            else:
                self.arrived()
            other = 1 - self.v

            @pl.loop(0, rows // 128)
            def _(step):
                here = pl.ds(pl.multiple_of(step * 128, 128), 128)

                def direct(first, right):
                    width = right.shape[0]
                    left = self.full[pl.ds(step * 8, 8), :, pl.ds(first, width)]
                    return jnp.dot(
                        left.reshape(128, width), right, preferred_element_type=F32
                    )

                def mirrored(left, right):
                    return lax.dot_general(
                        left.reshape(-1, 128),
                        right,
                        (((0,), (0,)), ((), ())),
                        preferred_element_type=F32,
                    )

                def columns(first):
                    return pl.ds(pl.multiple_of(first + step * 128, 128), 128)

                if self.kind == 0:
                    value = direct(0, normed[other, 0])
                    value += direct(rows, normed[other, 1, cross_rows(step // 2, core), :])
                    theirs = lax.rem(step // 2 + 1 - core, 2)
                    first = pl.multiple_of(lax.rem(step, 2) * 128, 128)
                    left = self.cross[pl.ds(theirs * 16, 16), :, pl.ds(first, 128)]
                    value += mirrored(left, normed[other, 1, cross_rows(theirs, 0), :])
                    acc[other, here, :] = value
                elif self.kind == 1:
                    value = direct(0, normed[other, pl.ds(2, 2)].reshape(2 * rows, rows))
                    for k in range(2):
                        left = self.full[:, :, columns(1024 + 512 * k)]
                        value += mirrored(left, normed[other, 6 + k])
                    acc[other, here, :] += value
                else:
                    value = direct(0, normed[other, 4 + turned])
                    left = self.full[:, :, columns(512)]
                    value += mirrored(left, normed[other, 5 - turned])
                    acc[other, here, :] += value

        def stages(self):
            steps = [self.product, self.pass_on, self.turn, self.reduced]
            if self.kind != 0:
                steps.append(self.spread)
            steps += [self.gather, self.gather_on]
            if self.kind == 0:
                steps.append(self.swap)
            return steps + [self.apply]

    same_items = []

    def diagonal():
        def step_sum(step, carry):
            here = pl.ds(pl.multiple_of(step * 64, 64), 64)
            both = normed[0, 0, here, :].astype(F32) * normed[1, 0, here, :].astype(F32)
            return carry + jnp.sum(both.reshape(8, 8, -1), axis=0)

        part = lax.fori_loop(0, rows // 64, step_sum, zero)
        same[batch] = part
        same_items.append(exchange(same))

    def unit_of(v, here):
        values = views[v][here, :].astype(F32)
        return (values - moments[pl.ds(2 * v, 1), :]) * moments[pl.ds(2 * v + 1, 1), :]

    def back_sums(v, last):
        def step_sum(step, carry):
            here = pl.ds(pl.multiple_of(step * 64, 64), 64)
            back = (2.0 * LAMBDA / total) * acc[v, here, :]
            back += extra * normed[1 - v, 0, here, :].astype(F32)
            acc[v, here, :] = back
            first = carry[0] + jnp.sum(back.reshape(8, 8, -1), axis=0)
            second = carry[1] + jnp.sum((back * unit_of(v, here)).reshape(8, 8, -1), axis=0)
            return first, second

        first, second = lax.fori_loop(0, rows // 64, step_sum, (zero, zero))
        last[batch, pl.ds(0, 1), :] = jnp.sum(first, axis=0, keepdims=True)
        last[batch, pl.ds(1, 1), :] = jnp.sum(second, axis=0, keepdims=True)
        last[batch, pl.ds(2, 6), :] = jnp.zeros((6, rows), F32)
        return exchange(last)

    def finish(v, last, items, out):
        both = collect(last, items) / total
        first, second = both[0:1], both[1:2]

        @pl.loop(0, rows // 64)
        def _(step):
            here = pl.ds(pl.multiple_of(step * 64, 64), 64)
            scale = moments[pl.ds(2 * v + 1, 1), :]
            value = scale * (acc[v, here, :] - first - unit_of(v, here) * second)
            out[here, :] = value.astype(BF16)

    start = {(1, 0): 0, (0, 0): 1, (1, 1): 2, (1, 2): 3, (0, 1): 5, (0, 2): 6}
    running = [(begin, Block(v, kind)) for (v, kind), begin in start.items()]
    ends = {(block.v, block.kind): begin + len(block.stages()) - 1 for begin, block in running}
    early = max(end for (v, _), end in ends.items() if v == 1)
    for tick in range(max(ends.values()) + 1):
        for begin, block in running:
            steps = block.stages()
            if 0 <= tick - begin < len(steps):
                steps[tick - begin]()
        if tick == 1:
            diagonal()
        if tick == early:
            cosine = jnp.sum(collect(same, same_items[0]), axis=0, keepdims=True) / total
            extra = (2.0 * (cosine - 1.0)).astype(BF16).astype(F32) - 2.0 * LAMBDA * cosine
            items_a = back_sums(0, last_a)
    items_b = back_sums(1, last_b)
    finish(0, last_a, items_a, ga)
    finish(1, last_b, items_b, gb)
    net.finish()
    assert (len(net.sends), net.receives) == (SENDS, RECEIVES)


def body(view_a, view_b):
    rows, width = view_a.shape
    total = rows * lax.axis_size("batch")
    blocks = []
    for _ in range(2):
        for columns, wide in zip(REDUCED, GATHERED):
            blocks += [
                pltpu.VMEM((32, 16, columns), BF16),
                pltpu.VMEM((2, 2, 2, 16, columns), BF16),
                pltpu.VMEM((2, 2, 4, 16, columns), BF16),
                pltpu.VMEM((2, 3, 16, columns), BF16),
                pltpu.VMEM((32, 16, wide), BF16),
            ]
    vmem = pl.BlockSpec(memory_space=pltpu.VMEM)
    return pl.pallas_call(
        functools.partial(kernel, rows, total),
        out_shape=(jax.ShapeDtypeStruct((rows, width), BF16),) * 2,
        in_specs=[vmem, vmem],
        out_specs=(vmem, vmem),
        scratch_shapes=[
            pltpu.VMEM((2, 8, rows, width), BF16),
            pltpu.VMEM((2, 8, rows, width), BF16),
            pltpu.VMEM((8, 8, width), F32),
            pltpu.VMEM((8, 8, width), F32),
            pltpu.VMEM((8, 8, width), F32),
            pltpu.VMEM((8, 8, width), F32),
            pltpu.VMEM((8, width), F32),
            pltpu.VMEM((2, rows, width), F32),
            pltpu.VMEM((2, 32, 16, 256), BF16),
            pltpu.SemaphoreType.DMA((SENDS,)),
            pltpu.SemaphoreType.DMA((RECEIVES,)),
        ]
        + blocks,
        compiler_params=pltpu.CompilerParams(
            collective_id=0, has_side_effects=True, vmem_limit_bytes=56 * 2**20
        ),
        name="gram_gradient",
    )(view_a, view_b)


def solution(mesh):
    return jax.shard_map(
        body,
        mesh=mesh,
        in_specs=(P("batch", "feat"), P("batch", "feat")),
        out_specs=(P("batch", "feat"), P("batch", "feat")),
        check_vma=False,
    )
```

time: 124 us -> 117 us (0.944)
  Pallas kernels: 120 us -> 114 us
    pallas_call x1, Pallas kernels: 120 us -> 114 us  [body(): pl.pallas_call(functools.partial(kernel, rows, total), out_shape=(jax.Sha...]
where the time goes in v3:
time: 117 us
  Pallas kernels  114 us (97%)
  local copies, waits for them, and re-layouts  2.72 us (2%)
    pallas_call x1, Pallas kernels, body(): pl.pallas_call(functools.partial(kernel, rows, total), out_shape=(jax.Sha...  114 us
    unnamed x4, local copies, waits for them, and re-layouts  2.72 us

profile of v3, /device:TPU:1, one launch (start us, length us, event | category | flops | bytes accessed | tf_op | source)
XLA Modules:
  0.0 116.9 jit_solution(18265384066796864705)
XLA Ops:
  0.6 113.5 %gram_gradient.1 = (bf16[512,512]{1,0:T(8,128)(2,1)}, bf16[512,512]{1,0:T(8,128)(2,1)}) custom-call(bf16[512,512]{1,0:T(8,128)(2,1)} %va.1, bf16[512,512]{1,0:T(8,128)(2,1)} %vb.1), custom_call_target="tpu_custom_call" | custom-call | tf_op jit(solution)/shard_map/gram_gradient/pallas_call | solution.py:479
  114.1 0.0 copy-start
  114.2 1.9 %copy.6 = bf16[512,512]{1,0:T(8,128)(2,1)} copy(bf16[512,512]{1,0:T(8,128)(2,1)} %get-tuple-element.4) | data formatting | bytes 1048576
  116.1 0.0 copy-done
  116.1 0.8 copy.7
Async XLA Ops:
  114.1 1.9 %copy-start = (bf16[512,512]{1,0:T(8,128)(2,1)S(1)}, bf16[512,512]{1,0:T(8,128)(2,1)}, u32[]{:S(2)}) copy-start(bf16[512,512]{1,0:T(8,128)(2,1)} %get-tuple-element.5) | copy-start | bytes 1572868

commit v4 on v3

--- a/solution.py
+++ b/solution.py
@@ -11,9 +11,18 @@
 MESH = pl.DeviceIdType.MESH
 F32 = jnp.float32
 BF16 = jnp.bfloat16
-SENDS, RECEIVES = 20, 60
+SENDS, RECEIVES = 22, 60
 REDUCED = (768, 1024, 512)
-GATHERED = (768, 2048, 1024)
+GATHERED = (768, 1024, 1024)
+ROWS = ((0, 1), (3,), (6, 8, 11, 15), (21, 24, 29, 31))
+BLOCKS = (
+    (1, 0, (4, 7, 12, 16, 23, 40, 49, 53)),
+    (0, 0, (2, 5, 9, 13, 19, 45, 48, 56)),
+    (1, 1, (10, 14, 18, 22, 27, 36, 43, 50)),
+    (1, 2, (17, 20, 26, 30, 33, 39, 51, 55)),
+    (0, 1, (25, 28, 34, 37, 42, 46, 52, 57)),
+    (0, 2, (32, 35, 38, 41, 44, 47, 54, 58)),
+)
 
 
 def rem4(value):
@@ -54,8 +63,8 @@
 
 
 def kernel(rows, total, va, vb, ga, gb, *scratch):
-    (raw, normed, stat, same, last_a, last_b, moments, acc, cross, send_sems, recv_sems) = scratch[:11]
-    blocks = scratch[11:]
+    (raw, normed, stat, same, last_a, last_b, moments, acc, cross, back, send_sems, recv_sems) = scratch[:12]
+    blocks = scratch[12:]
     net = Net(send_sems, recv_sems)
     views = (va, vb)
     batch, feat = lax.axis_index("batch"), lax.axis_index("feat")
@@ -157,6 +166,8 @@
         send_rows(v, raw.at[v, 6], 7, sibling)
         if v == 1:
             send_near(0)
+
+    def take_near(v):
         normalize(v, 2)
         normalize(v, 6)
         for slot in (3, 7):
@@ -166,25 +177,37 @@
     def far_rows(v):
         wait_rows(v, 4)
         send_rows(v, raw.at[v, 4], 5, sibling)
+
+    def take_far(v):
         normalize(v, 4)
         wait_rows(v, 5)
         normalize(v, 5)
 
     net.cross_sends = [net.sender(cross.at[v]) for v in range(2)]
+    net.back_sends = [net.sender(back.at[v]) for v in range(2)]
+    begun = set()
 
     def cross_rows(part, turn):
         return pl.ds(pl.multiple_of(lax.rem(part + turn, 2) * 256, 256), 256)
 
     turned = x // 2
+
+    def mirrored(left, right):
+        return lax.dot_general(
+            left.reshape(-1, 128), right, (((0,), (0,)), ((), ())), preferred_element_type=F32
+        )
+
+    def add(v, here, value):
+        acc[v, here, :] = acc[v, here, :] + value if v in begun else value
 
     class Block:
         def __init__(self, v, kind):
             self.v, self.kind = v, kind
             base = (v * 3 + kind) * 5
             self.part, self.r1, self.r2, self.r3, self.full = blocks[base : base + 5]
-            self.cross = cross.at[v]
+            self.cross, self.back = cross.at[v], back.at[v]
             self.columns = REDUCED[kind]
-            mirrored = 0 if kind == 0 else 1
+            mirrored = 1 if kind == 2 else 0
             self.reduce_send = net.sender(self.part.at[pl.ds(0, 30)])
             self.gather_send = net.sender(self.full.at[pl.ds(0, 30 + mirrored)])
             self.sems = [net.receiver() for _ in range(7)]
@@ -194,13 +217,6 @@
 
         def product(self):
             v = self.v
-            if self.kind == 0:
-                own_rows(v)
-            elif self.kind == 1:
-                near_rows(v)
-            else:
-                far_rows(v)
-
             @pl.loop(0, rows // 128)
             def _(step):
                 left = normed[v, 0, pl.ds(pl.multiple_of(step * 128, 128), 128), :]
@@ -218,7 +234,8 @@
                     block(0, normed[v, 0])
                     block(rows, normed[v, 1, cross_rows(step // 2, core), :])
                 elif self.kind == 1:
-                    block(0, normed[v, pl.ds(2, 2)].reshape(2 * rows, rows))
+                    block(0, normed[v, 2])
+                    block(rows, normed[v, 7])
                 else:
                     block(0, normed[v, 4 + turned])
 
@@ -293,21 +310,30 @@
                 for k in range(3):
                     value = value + self.r3[half, k].astype(F32)
                 self.full[own, :, pl.ds(0, self.columns)] = value.astype(BF16)
-                if self.kind == 1:
-                    for k in range(2):
-                        self.mirror(own, 512 * k, 1024 + 512 * k, at_batch(1, k))
                 if self.kind == 2:
                     self.mirror(own, 0, 512, at_batch(2, turned))
-            if self.kind == 0:
+            if self.kind != 2:
                 self.spread()
 
         def spread(self):
-            if self.kind != 0:
+            if self.kind == 2:
                 wait(self.sems[3], self.full.at[pl.ds(0, 1)])
             for half in range(2):
                 here = self.full.at[self.own(half)]
                 for k in range(1, 4):
                     send(here, here, self.gather_send, self.sems[4], at_feat(half, 0, k))
+
+        def send_back(self, half, ahead, first, count):
+            m1, _ = self.mine(half)
+            chunks = pl.ds(half * 16 + rem4(m1 + ahead) * 4 + first, count)
+            for k, device in enumerate((at_batch(1, 0), at_batch(3, 1))):
+                send(
+                    self.full.at[chunks, :, pl.ds(512 * k, 512)],
+                    self.back.at[k, chunks],
+                    net.back_sends[self.v],
+                    self.sems[3],
+                    device,
+                )
 
         def gather(self):
             wait(self.sems[4], self.full.at[pl.ds(0, 6)])
@@ -316,6 +342,8 @@
                 here = self.full.at[pl.ds(half * 16 + m1 * 4, 4)]
                 for k in range(2):
                     send(here, here, self.gather_send, self.sems[5], at_feat(half, 1 + 2 * k, 0))
+                if self.kind == 1:
+                    self.send_back(half, 0, 0, 4)
 
         def gather_on(self):
             wait(self.sems[5], self.full.at[pl.ds(0, 16)])
@@ -325,9 +353,14 @@
                     base = half * 16 + rem4(m1 + 3 + 2 * k) * 4
                     here = self.full.at[pl.ds(base + 2 * k, 2)]
                     send(here, here, self.gather_send, self.sems[6], at_feat(half, 1 + 2 * k, 0))
+                    if self.kind == 1:
+                        self.send_back(half, 3 + 2 * k, 0, 4)
 
         def arrived(self):
             wait(self.sems[6], self.full.at[pl.ds(0, 8)])
+            if self.kind == 1:
+                for half in range(2):
+                    self.send_back(half, 2, 0, 4)
 
         def swap(self):
             self.arrived()
@@ -357,14 +390,6 @@
                         left.reshape(128, width), right, preferred_element_type=F32
                     )
 
-                def mirrored(left, right):
-                    return lax.dot_general(
-                        left.reshape(-1, 128),
-                        right,
-                        (((0,), (0,)), ((), ())),
-                        preferred_element_type=F32,
-                    )
-
                 def columns(first):
                     return pl.ds(pl.multiple_of(first + step * 128, 128), 128)
 
@@ -375,29 +400,39 @@
                     first = pl.multiple_of(lax.rem(step, 2) * 128, 128)
                     left = self.cross[pl.ds(theirs * 16, 16), :, pl.ds(first, 128)]
                     value += mirrored(left, normed[other, 1, cross_rows(theirs, 0), :])
-                    acc[other, here, :] = value
                 elif self.kind == 1:
-                    value = direct(0, normed[other, pl.ds(2, 2)].reshape(2 * rows, rows))
-                    for k in range(2):
-                        left = self.full[:, :, columns(1024 + 512 * k)]
-                        value += mirrored(left, normed[other, 6 + k])
-                    acc[other, here, :] += value
+                    value = direct(0, normed[other, 2]) + direct(rows, normed[other, 7])
                 else:
                     value = direct(0, normed[other, 4 + turned])
                     left = self.full[:, :, columns(512)]
                     value += mirrored(left, normed[other, 5 - turned])
-                    acc[other, here, :] += value
+                add(other, here, value)
+
+            begun.add(other)
+
+        def apply_back(self):
+            wait(self.sems[3], self.back)
+            other = 1 - self.v
+
+            @pl.loop(0, rows // 128)
+            def _(step):
+                here = pl.ds(pl.multiple_of(step * 128, 128), 128)
+                value = mirrored(self.back[0, :, :, here], normed[other, 6])
+                value += mirrored(self.back[1, :, :, here], normed[other, 3])
+                add(other, here, value)
+
+            begun.add(other)
 
         def stages(self):
-            steps = [self.product, self.pass_on, self.turn, self.reduced]
-            if self.kind != 0:
-                steps.append(self.spread)
-            steps += [self.gather, self.gather_on]
+            reduce = [self.product, self.pass_on, self.turn, self.reduced]
             if self.kind == 0:
-                steps.append(self.swap)
-            return steps + [self.apply]
+                return reduce + [self.gather, self.gather_on, self.swap, self.apply]
+            if self.kind == 1:
+                return reduce + [self.gather, self.gather_on, self.apply, self.apply_back]
+            return reduce + [self.spread, self.gather, self.gather_on, self.apply]
 
     same_items = []
+    extras = []
 
     def diagonal():
         def step_sum(step, carry):
@@ -417,7 +452,7 @@
         def step_sum(step, carry):
             here = pl.ds(pl.multiple_of(step * 64, 64), 64)
             back = (2.0 * LAMBDA / total) * acc[v, here, :]
-            back += extra * normed[1 - v, 0, here, :].astype(F32)
+            back += extras[0] * normed[1 - v, 0, here, :].astype(F32)
             acc[v, here, :] = back
             first = carry[0] + jnp.sum(back.reshape(8, 8, -1), axis=0)
             second = carry[1] + jnp.sum((back * unit_of(v, here)).reshape(8, 8, -1), axis=0)
@@ -440,23 +475,29 @@
             value = scale * (acc[v, here, :] - first - unit_of(v, here) * second)
             out[here, :] = value.astype(BF16)
 
-    start = {(1, 0): 0, (0, 0): 1, (1, 1): 2, (1, 2): 3, (0, 1): 5, (0, 2): 6}
-    running = [(begin, Block(v, kind)) for (v, kind), begin in start.items()]
-    ends = {(block.v, block.kind): begin + len(block.stages()) - 1 for begin, block in running}
-    early = max(end for (v, _), end in ends.items() if v == 1)
-    for tick in range(max(ends.values()) + 1):
-        for begin, block in running:
-            steps = block.stages()
-            if 0 <= tick - begin < len(steps):
-                steps[tick - begin]()
-        if tick == 1:
-            diagonal()
-        if tick == early:
-            cosine = jnp.sum(collect(same, same_items[0]), axis=0, keepdims=True) / total
-            extra = (2.0 * (cosine - 1.0)).astype(BF16).astype(F32) - 2.0 * LAMBDA * cosine
-            items_a = back_sums(0, last_a)
+    plan = []
+
+    def add_rows(name, ticks):
+        plan.extend(zip(ticks, name))
+
+    add_rows([lambda v=v: own_rows(v) for v in (1, 0)], ROWS[0])
+    add_rows([diagonal], ROWS[1])
+    for n, v in enumerate((1, 0)):
+        steps = [lambda v=v, f=f: f(v) for f in (near_rows, take_near, far_rows, take_far)]
+        add_rows(steps, ROWS[2 + n])
+    for v, kind, ticks in BLOCKS:
+        add_rows(Block(v, kind).stages(), ticks)
+    def early():
+        cosine = jnp.sum(collect(same, same_items[0]), axis=0, keepdims=True) / total
+        extra = (2.0 * (cosine - 1.0)).astype(BF16).astype(F32) - 2.0 * LAMBDA * cosine
+        extras.append(extra)
+        extras.append(back_sums(0, last_a))
+
+    add_rows([early], (max(ticks[-1] for v, _, ticks in BLOCKS if v == 1),))
+    for _, step in sorted(plan, key=lambda item: item[0]):
+        step()
     items_b = back_sums(1, last_b)
-    finish(0, last_a, items_a, ga)
+    finish(0, last_a, extras[1], ga)
     finish(1, last_b, items_b, gb)
     net.finish()
     assert (len(net.sends), net.receives) == (SENDS, RECEIVES)
@@ -491,6 +532,7 @@
             pltpu.VMEM((8, width), F32),
             pltpu.VMEM((2, rows, width), F32),
             pltpu.VMEM((2, 32, 16, 256), BF16),
+            pltpu.VMEM((2, 2, 32, 16, 512), BF16),
             pltpu.SemaphoreType.DMA((SENDS,)),
             pltpu.SemaphoreType.DMA((RECEIVES,)),
         ]

time: 117 us -> 98.6 us (0.84)
  Pallas kernels: 114 us -> 95.1 us
    pallas_call x1, Pallas kernels: 114 us -> 95.1 us  [body(): pl.pallas_call(functools.partial(kernel, rows, total), out_shape=(jax.Sha...]
where the time goes in v4:
time: 98.6 us; the launch traced here: 98.5 us
  Pallas kernels  95.1 us (96%)
  local copies, waits for them, and re-layouts  2.72 us (3%)
    pallas_call x1, Pallas kernels, body(): pl.pallas_call(functools.partial(kernel, rows, total), out_shape=(jax.Sha...  95.1 us
    unnamed x4, local copies, waits for them, and re-layouts  2.72 us

profile of v4, /device:TPU:1, one launch (start us, length us, event | category | flops | bytes accessed | tf_op | source)
XLA Modules:
  0.0 98.5 jit_solution(1212280067009625373)
XLA Ops:
  0.6 95.1 %gram_gradient.1 = (bf16[512,512]{1,0:T(8,128)(2,1)}, bf16[512,512]{1,0:T(8,128)(2,1)}) custom-call(bf16[512,512]{1,0:T(8,128)(2,1)} %va.1, bf16[512,512]{1,0:T(8,128)(2,1)} %vb.1), custom_call_target="tpu_custom_call" | custom-call | tf_op jit(solution)/shard_map/gram_gradient/pallas_call | solution.py:520
  95.7 0.0 copy-start
  95.7 1.9 %copy.6 = bf16[512,512]{1,0:T(8,128)(2,1)} copy(bf16[512,512]{1,0:T(8,128)(2,1)} %get-tuple-element.4) | data formatting | bytes 1048576
  97.7 0.0 copy-done
  97.7 0.8 copy.7
Async XLA Ops:
  95.7 1.9 %copy-start = (bf16[512,512]{1,0:T(8,128)(2,1)S(1)}, bf16[512,512]{1,0:T(8,128)(2,1)}, u32[]{:S(2)}) copy-start(bf16[512,512]{1,0:T(8,128)(2,1)} %get-tuple-element.5) | copy-start | bytes 1572868

commit v5 on v4

--- a/solution.py
+++ b/solution.py
@@ -12,16 +12,16 @@
 F32 = jnp.float32
 BF16 = jnp.bfloat16
 SENDS, RECEIVES = 22, 60
-REDUCED = (768, 1024, 512)
-GATHERED = (768, 1024, 1024)
-ROWS = ((0, 1), (3,), (6, 8, 11, 15), (21, 24, 29, 31))
+REDUCED = (640, 1024, 512)
+GATHERED = (640, 1024, 1024)
+ROWS = ((0, 1), (2,), (7, 8, 14, 22, 26), (16, 20, 17, 30, 32))
 BLOCKS = (
-    (1, 0, (4, 7, 12, 16, 23, 40, 49, 53)),
-    (0, 0, (2, 5, 9, 13, 19, 45, 48, 56)),
-    (1, 1, (10, 14, 18, 22, 27, 36, 43, 50)),
-    (1, 2, (17, 20, 26, 30, 33, 39, 51, 55)),
-    (0, 1, (25, 28, 34, 37, 42, 46, 52, 57)),
-    (0, 2, (32, 35, 38, 41, 44, 47, 54, 58)),
+    (1, 0, (5, 6, 11, 15, 41, 46, 49, 56)),
+    (0, 0, (3, 4, 9, 12, 19, 23, 27, 36)),
+    (1, 1, (10, 13, 18, 24, 29, 35, 40, 52)),
+    (1, 2, (28, 34, 38, 43, 47, 51, 55, 59)),
+    (0, 1, (21, 25, 31, 39, 44, 48, 53, 58)),
+    (0, 2, (33, 37, 42, 45, 50, 54, 57, 60)),
 )
 
 
@@ -78,7 +78,7 @@
         dy, dz = (d1, d2) if half == 0 else (d2, d1)
         return (batch, rem4(y + dy) * 4 + rem4(z + dz))
 
-    peers = [(lax.rem(batch + k, 8), feat) for k in range(1, 8)]
+    peers = [(lax.rem(batch + k, 8), feat) for k in (4, 3, 5, 2, 6, 1, 7)]
     planes = [at_feat(half, k, 0) for half in range(2) for k in range(1, 4)]
     barrier = pltpu.get_barrier_semaphore()
     for device in peers + planes:
@@ -100,20 +100,21 @@
 
     pl.semaphore_wait(barrier, len(peers) + len(planes))
 
-    def exchange(ref):
-        sender, receiver = net.sender(ref.at[pl.ds(0, 7)]), net.receiver()
+    def exchange(ref, count=8):
+        used = pl.ds(0, count)
+        sender, receiver = net.sender(ref.at[pl.ds(0, 7), used]), net.receiver()
         for device in peers:
-            send(ref.at[batch], ref.at[batch], sender, receiver, device)
+            send(ref.at[batch, used], ref.at[batch, used], sender, receiver, device)
         return receiver
 
-    def collect(ref, receiver):
-        wait(receiver, ref.at[pl.ds(0, 7)])
+    def collect(ref, receiver, count=8):
+        wait(receiver, ref.at[pl.ds(0, 7), pl.ds(0, count)])
         result = ref[0]
         for k in range(1, 8):
             result = result + ref[k]
         return result
 
-    stat_items = exchange(stat)
+    stat_items = exchange(stat, 4)
     sibling = (batch + 1 - 2 * core, feat)
     half = rows // 2
     upper, lower = pl.ds(0, half), pl.ds(half, half)
@@ -135,7 +136,7 @@
     for v in (1, 0):
         send_rows(v, views[v], 1, sibling)
 
-    sum_all = collect(stat, stat_items)
+    sum_all = collect(stat, stat_items, 4)
     for v in range(2):
         mean = sum_all[2 * v : 2 * v + 1] / total
         square = sum_all[2 * v + 1 : 2 * v + 2] / total
@@ -160,8 +161,6 @@
     def near_rows(v):
         wait_rows(v, 6)
         wait_rows(v, 2)
-        send_rows(v, raw.at[v, 6, upper], 4, at_batch(1, 0), upper)
-        send_rows(v, raw.at[v, 2, lower], 4, at_batch(3, 0), lower)
         send_rows(v, raw.at[v, 2], 3, sibling)
         send_rows(v, raw.at[v, 6], 7, sibling)
         if v == 1:
@@ -174,6 +173,10 @@
             wait_rows(v, slot)
             normalize(v, slot)
 
+    def pass_far(v):
+        send_rows(v, raw.at[v, 6, upper], 4, at_batch(1, 0), upper)
+        send_rows(v, raw.at[v, 2, lower], 4, at_batch(3, 0), lower)
+
     def far_rows(v):
         wait_rows(v, 4)
         send_rows(v, raw.at[v, 4], 5, sibling)
@@ -189,6 +192,12 @@
 
     def cross_rows(part, turn):
         return pl.ds(pl.multiple_of(lax.rem(part + turn, 2) * 256, 256), 256)
+
+    def tile(step):
+        return pl.ds(pl.multiple_of(step * 128, 128), 128)
+
+    def partner(step):
+        return rem4(step + 2 + (step // 2) * (1 + 2 * lax.rem(step, 2)))
 
     turned = x // 2
 
@@ -231,8 +240,9 @@
                     ).reshape(8, 16, width)
 
                 if self.kind == 0:
-                    block(0, normed[v, 0])
-                    block(rows, normed[v, 1, cross_rows(step // 2, core), :])
+                    block(0, normed[v, 0, cross_rows(step // 2, 0), :])
+                    block(256, normed[v, 0, tile(partner(step)), :])
+                    block(384, normed[v, 1, cross_rows(step // 2, core), :])
                 elif self.kind == 1:
                     block(0, normed[v, 2])
                     block(rows, normed[v, 7])
@@ -365,7 +375,7 @@
         def swap(self):
             self.arrived()
             send(
-                self.full.at[:, :, pl.ds(rows, rows // 2)],
+                self.full.at[:, :, pl.ds(384, 256)],
                 self.cross,
                 net.cross_sends[self.v],
                 self.sems[3],
@@ -394,8 +404,12 @@
                     return pl.ds(pl.multiple_of(first + step * 128, 128), 128)
 
                 if self.kind == 0:
-                    value = direct(0, normed[other, 0])
-                    value += direct(rows, normed[other, 1, cross_rows(step // 2, core), :])
+                    value = direct(0, normed[other, 0, cross_rows(step // 2, 0), :])
+                    value += direct(256, normed[other, 0, tile(partner(step)), :])
+                    value += direct(384, normed[other, 1, cross_rows(step // 2, core), :])
+                    taker = 3 - step + (step // 2) * (2 * step - 5)
+                    left = self.full[pl.ds(taker * 8, 8), :, pl.ds(256, 128)]
+                    value += mirrored(left, normed[other, 0, tile(taker), :])
                     theirs = lax.rem(step // 2 + 1 - core, 2)
                     first = pl.multiple_of(lax.rem(step, 2) * 128, 128)
                     left = self.cross[pl.ds(theirs * 16, 16), :, pl.ds(first, 128)]
@@ -462,10 +476,10 @@
         last[batch, pl.ds(0, 1), :] = jnp.sum(first, axis=0, keepdims=True)
         last[batch, pl.ds(1, 1), :] = jnp.sum(second, axis=0, keepdims=True)
         last[batch, pl.ds(2, 6), :] = jnp.zeros((6, rows), F32)
-        return exchange(last)
+        return exchange(last, 2)
 
     def finish(v, last, items, out):
-        both = collect(last, items) / total
+        both = collect(last, items, 2) / total
         first, second = both[0:1], both[1:2]
 
         @pl.loop(0, rows // 64)
@@ -483,7 +497,7 @@
     add_rows([lambda v=v: own_rows(v) for v in (1, 0)], ROWS[0])
     add_rows([diagonal], ROWS[1])
     for n, v in enumerate((1, 0)):
-        steps = [lambda v=v, f=f: f(v) for f in (near_rows, take_near, far_rows, take_far)]
+        steps = [lambda v=v, f=f: f(v) for f in (near_rows, take_near, pass_far, far_rows, take_far)]
         add_rows(steps, ROWS[2 + n])
     for v, kind, ticks in BLOCKS:
         add_rows(Block(v, kind).stages(), ticks)
@@ -519,7 +533,7 @@
     vmem = pl.BlockSpec(memory_space=pltpu.VMEM)
     return pl.pallas_call(
         functools.partial(kernel, rows, total),
-        out_shape=(jax.ShapeDtypeStruct((rows, width), BF16),) * 2,
+        out_shape=(pltpu.VMEM((rows, width), BF16),) * 2,
         in_specs=[vmem, vmem],
         out_specs=(vmem, vmem),
         scratch_shapes=[

time: 98.6 us -> 93.3 us (0.946)
  Pallas kernels: 95.1 us -> 91 us
  local copies, waits for them, and re-layouts: 2.72 us -> 1.59 us
    pallas_call x1, Pallas kernels: 95.1 us -> 91 us  [body(): pl.pallas_call(functools.partial(kernel, rows, total), out_shape=(pltpu.V...]
    unnamed x4 -> x2, local copies, waits for them, and re-layouts: 2.72 us -> 1.59 us
where the time goes in v5:
time: 93.3 us; the launch traced here: 93.2 us
  Pallas kernels  91 us (98%)
  local copies, waits for them, and re-layouts  1.59 us (2%)
    pallas_call x1, Pallas kernels, body(): pl.pallas_call(functools.partial(kernel, rows, total), out_shape=(pltpu.V...  91 us

profile of v5, /device:TPU:1, one launch (start us, length us, event | category | flops | bytes accessed | tf_op | source)
XLA Modules:
  0.0 93.2 jit_solution(4812971590826214378)
XLA Ops:
  0.6 91.0 %gram_gradient.1 = (bf16[512,512]{1,0:T(8,128)(2,1)S(1)}, bf16[512,512]{1,0:T(8,128)(2,1)S(1)}) custom-call(bf16[512,512]{1,0:T(8,128)(2,1)} %va.1, bf16[512,512]{1,0:T(8,128)(2,1)} %vb.1), custom_call_target="tpu_custom_call" | custom-call | tf_op jit(solution)/shard_map/gram_gradient/pallas_call | solution.py:534
  91.6 0.8 copy.6
  92.4 0.8 copy.7

commit v6 on v5

--- a/solution.py
+++ b/solution.py
@@ -14,14 +14,14 @@
 SENDS, RECEIVES = 22, 60
 REDUCED = (640, 1024, 512)
 GATHERED = (640, 1024, 1024)
-ROWS = ((0, 1), (2,), (7, 8, 14, 22, 26), (16, 20, 17, 30, 32))
+ROWS = ((0, 1), (20,), (5, 6, 8, 23, 27), (13, 17, 14, 26, 30))
 BLOCKS = (
-    (1, 0, (5, 6, 11, 15, 41, 46, 49, 56)),
-    (0, 0, (3, 4, 9, 12, 19, 23, 27, 36)),
-    (1, 1, (10, 13, 18, 24, 29, 35, 40, 52)),
-    (1, 2, (28, 34, 38, 43, 47, 51, 55, 59)),
-    (0, 1, (21, 25, 31, 39, 44, 48, 53, 58)),
-    (0, 2, (33, 37, 42, 45, 50, 54, 57, 60)),
+    (1, 0, (2, 3, 7, 11, 16, 21, 36, 40)),
+    (0, 0, (4, 10, 15, 22, 39, 45, 51, 56)),
+    (1, 1, (9, 12, 18, 24, 28, 33, 41, 54)),
+    (1, 2, (29, 34, 38, 43, 47, 50, 55, 59)),
+    (0, 1, (19, 25, 31, 37, 44, 48, 53, 58)),
+    (0, 2, (32, 35, 42, 46, 49, 52, 57, 60)),
 )
 
 
@@ -62,11 +62,17 @@
     pltpu.make_async_copy(moved, moved, sem).wait()
 
 
-def kernel(rows, total, va, vb, ga, gb, *scratch):
-    (raw, normed, stat, same, last_a, last_b, moments, acc, cross, back, send_sems, recv_sems) = scratch[:12]
-    blocks = scratch[12:]
+def kernel(rows, total, far_a, far_b, ga, gb, moments, *scratch):
+    (raw, normed, stat, same, last_a, last_b, acc, cross, back, own, own_sems, send_sems, recv_sems) = scratch[:13]
+    blocks = scratch[13:]
     net = Net(send_sems, recv_sems)
-    views = (va, vb)
+    views = (own.at[0], own.at[1])
+    loads = [
+        pltpu.make_async_copy(source, own.at[v], own_sems.at[v])
+        for v, source in enumerate((far_a, far_b))
+    ]
+    for load in loads:
+        load.start()
     batch, feat = lax.axis_index("batch"), lax.axis_index("feat")
     x, core = batch // 2, lax.rem(batch, 2)
     y, z = feat // 4, rem4(feat)
@@ -93,6 +99,8 @@
         return tuple(out)
 
     zero = jnp.zeros((8, rows), F32)
+    for load in loads:
+        load.wait()
     parts = lax.fori_loop(0, rows // 64, sums, (zero,) * 4)
     for k in range(4):
         stat[batch, pl.ds(k, 1), :] = jnp.sum(parts[k], axis=0, keepdims=True)
@@ -135,6 +143,7 @@
     send_near(1)
     for v in (1, 0):
         send_rows(v, views[v], 1, sibling)
+    send_near(0)
 
     sum_all = collect(stat, stat_items, 4)
     for v in range(2):
@@ -163,8 +172,6 @@
         wait_rows(v, 2)
         send_rows(v, raw.at[v, 2], 3, sibling)
         send_rows(v, raw.at[v, 6], 7, sibling)
-        if v == 1:
-            send_near(0)
 
     def take_near(v):
         normalize(v, 2)
@@ -203,7 +210,7 @@
 
     def mirrored(left, right):
         return lax.dot_general(
-            left.reshape(-1, 128), right, (((0,), (0,)), ((), ())), preferred_element_type=F32
+            left.reshape(-1, left.shape[-1]), right, (((0,), (0,)), ((), ())), preferred_element_type=F32
         )
 
     def add(v, here, value):
@@ -388,7 +395,32 @@
             else:
                 self.arrived()
             other = 1 - self.v
-
+            if self.kind == 0:
+                self.apply_own(other)
+            else:
+
+                @pl.loop(0, 2)
+                def _(step):
+                    here = pl.ds(pl.multiple_of(step * 256, 256), 256)
+
+                    def direct(first, right):
+                        left = self.full[pl.ds(step * 16, 16), :, pl.ds(first, 512)]
+                        return jnp.dot(
+                            left.reshape(256, 512), right, preferred_element_type=F32
+                        )
+
+                    if self.kind == 1:
+                        value = direct(0, normed[other, 2]) + direct(rows, normed[other, 7])
+                    else:
+                        value = direct(0, normed[other, 4 + turned])
+                        columns = pl.ds(pl.multiple_of(512 + step * 256, 256), 256)
+                        left = self.full[:, :, columns]
+                        value += mirrored(left, normed[other, 5 - turned])
+                    add(other, here, value)
+
+            begun.add(other)
+
+        def apply_own(self, other):
             @pl.loop(0, rows // 128)
             def _(step):
                 here = pl.ds(pl.multiple_of(step * 128, 128), 128)
@@ -400,37 +432,25 @@
                         left.reshape(128, width), right, preferred_element_type=F32
                     )
 
-                def columns(first):
-                    return pl.ds(pl.multiple_of(first + step * 128, 128), 128)
-
-                if self.kind == 0:
-                    value = direct(0, normed[other, 0, cross_rows(step // 2, 0), :])
-                    value += direct(256, normed[other, 0, tile(partner(step)), :])
-                    value += direct(384, normed[other, 1, cross_rows(step // 2, core), :])
-                    taker = 3 - step + (step // 2) * (2 * step - 5)
-                    left = self.full[pl.ds(taker * 8, 8), :, pl.ds(256, 128)]
-                    value += mirrored(left, normed[other, 0, tile(taker), :])
-                    theirs = lax.rem(step // 2 + 1 - core, 2)
-                    first = pl.multiple_of(lax.rem(step, 2) * 128, 128)
-                    left = self.cross[pl.ds(theirs * 16, 16), :, pl.ds(first, 128)]
-                    value += mirrored(left, normed[other, 1, cross_rows(theirs, 0), :])
-                elif self.kind == 1:
-                    value = direct(0, normed[other, 2]) + direct(rows, normed[other, 7])
-                else:
-                    value = direct(0, normed[other, 4 + turned])
-                    left = self.full[:, :, columns(512)]
-                    value += mirrored(left, normed[other, 5 - turned])
+                value = direct(0, normed[other, 0, cross_rows(step // 2, 0), :])
+                value += direct(256, normed[other, 0, tile(partner(step)), :])
+                value += direct(384, normed[other, 1, cross_rows(step // 2, core), :])
+                taker = 3 - step + (step // 2) * (2 * step - 5)
+                left = self.full[pl.ds(taker * 8, 8), :, pl.ds(256, 128)]
+                value += mirrored(left, normed[other, 0, tile(taker), :])
+                theirs = lax.rem(step // 2 + 1 - core, 2)
+                first = pl.multiple_of(lax.rem(step, 2) * 128, 128)
+                left = self.cross[pl.ds(theirs * 16, 16), :, pl.ds(first, 128)]
+                value += mirrored(left, normed[other, 1, cross_rows(theirs, 0), :])
                 add(other, here, value)
-
-            begun.add(other)
 
         def apply_back(self):
             wait(self.sems[3], self.back)
             other = 1 - self.v
 
-            @pl.loop(0, rows // 128)
+            @pl.loop(0, 2)
             def _(step):
-                here = pl.ds(pl.multiple_of(step * 128, 128), 128)
+                here = pl.ds(pl.multiple_of(step * 256, 256), 256)
                 value = mirrored(self.back[0, :, :, here], normed[other, 6])
                 value += mirrored(self.back[1, :, :, here], normed[other, 3])
                 add(other, here, value)
@@ -485,9 +505,7 @@
         @pl.loop(0, rows // 64)
         def _(step):
             here = pl.ds(pl.multiple_of(step * 64, 64), 64)
-            scale = moments[pl.ds(2 * v + 1, 1), :]
-            value = scale * (acc[v, here, :] - first - unit_of(v, here) * second)
-            out[here, :] = value.astype(BF16)
+            out[here, :] = acc[v, here, :] - first - unit_of(v, here) * second
 
     plan = []
 
@@ -531,11 +549,11 @@
                 pltpu.VMEM((32, 16, wide), BF16),
             ]
     vmem = pl.BlockSpec(memory_space=pltpu.VMEM)
-    return pl.pallas_call(
+    left_a, left_b, moments = pl.pallas_call(
         functools.partial(kernel, rows, total),
-        out_shape=(pltpu.VMEM((rows, width), BF16),) * 2,
-        in_specs=[vmem, vmem],
-        out_specs=(vmem, vmem),
+        out_shape=(pltpu.VMEM((rows, width), F32),) * 2 + (pltpu.VMEM((8, width), F32),),
+        in_specs=[pl.BlockSpec(memory_space=pl.ANY)] * 2,
+        out_specs=(vmem, vmem, vmem),
         scratch_shapes=[
             pltpu.VMEM((2, 8, rows, width), BF16),
             pltpu.VMEM((2, 8, rows, width), BF16),
@@ -543,10 +561,11 @@
             pltpu.VMEM((8, 8, width), F32),
             pltpu.VMEM((8, 8, width), F32),
             pltpu.VMEM((8, 8, width), F32),
-            pltpu.VMEM((8, width), F32),
             pltpu.VMEM((2, rows, width), F32),
             pltpu.VMEM((2, 32, 16, 256), BF16),
             pltpu.VMEM((2, 2, 32, 16, 512), BF16),
+            pltpu.VMEM((2, rows, width), BF16),
+            pltpu.SemaphoreType.DMA((2,)),
             pltpu.SemaphoreType.DMA((SENDS,)),
             pltpu.SemaphoreType.DMA((RECEIVES,)),
         ]
@@ -556,6 +575,7 @@
         ),
         name="gram_gradient",
     )(view_a, view_b)
+    return (moments[1] * left_a).astype(BF16), (moments[3] * left_b).astype(BF16)
 
 
 def solution(mesh):

time: 93.3 us -> 90.2 us (0.967)
  Pallas kernels: 91 us -> 88.1 us
  local copies, waits for them, and re-layouts: 1.59 us -> 0.01 us
  other arithmetic: 0 us -> 1.24 us
    pallas_call x1, Pallas kernels: 91 us -> 88.1 us  [body(): pl.pallas_call(functools.partial(kernel, rows, total), out_shape=(pltpu.V...]
    unnamed x2 -> x0, local copies, waits for them, and re-layouts: 1.59 us -> none
    convert_element_type x0 -> x1, other arithmetic: none -> 1.24 us  [body(): (moments[3] * left_b).astype(BF16)]
where the time goes in v6:
time: 90.2 us; the launch traced here: 90 us
  Pallas kernels  88.1 us (98%)
  other arithmetic  1.24 us (1%)
    pallas_call x1, Pallas kernels, body(): pl.pallas_call(functools.partial(kernel, rows, total), out_shape=(pltpu.V...  88.1 us

profile of v6, /device:TPU:1, one launch (start us, length us, event | category | flops | bytes accessed | tf_op | source)
XLA Modules:
  0.0 90.0 jit_solution(6923656381200421245)
XLA Ops:
  0.6 88.1 %gram_gradient.1 = (f32[512,512]{1,0:T(8,128)S(1)}, f32[512,512]{1,0:T(8,128)S(1)}, f32[8,512]{1,0:T(8,128)S(1)}) custom-call(bf16[512,512]{1,0:T(8,128)(2,1)} %far_a.1, bf16[512,512]{1,0:T(8,128)(2,1)} %far_b.1), custom_call_target="tpu_custom_call" | custom-call | tf_op jit(solution)/shard_map/gram_gradient/pallas_call | solution.py:552
  88.8 1.2 %multiply_convert_fusion = (bf16[512,512]{1,0:T(8,128)(2,1)}, bf16[512,512]{1,0:T(8,128)(2,1)}) fusion(f32[512,512]{1,0:T(8,128)S(1)} %get-tuple-element.7, f32[512]{0:T(512)S(1)} %bitcast.2, f32[512,512]{1,0:T(8,128)S(1)} %get-tuple-element.6, f32[512]{0:T(512)S(1)} %bitcast.3), kind=kLoop, calls=%fused_computation | loop fusion | flops 1048576 | bytes 3149824 | tf_op jit(solution)/shard_map/convert_element_type | solution.py:578
  (1 shorter events, 0.0 us)

commit v7 on v6

--- a/solution.py
+++ b/solution.py
@@ -14,14 +14,14 @@
 SENDS, RECEIVES = 22, 60
 REDUCED = (640, 1024, 512)
 GATHERED = (640, 1024, 1024)
-ROWS = ((0, 1), (20,), (5, 6, 8, 23, 27), (13, 17, 14, 26, 30))
+ROWS = ((0, 1), (16,), (5, 6, 8, 23, 27), (13, 18, 14, 26, 30))
 BLOCKS = (
-    (1, 0, (2, 3, 7, 11, 16, 21, 36, 40)),
+    (1, 0, (2, 3, 7, 11, 17, 21, 36, 42)),
     (0, 0, (4, 10, 15, 22, 39, 45, 51, 56)),
-    (1, 1, (9, 12, 18, 24, 28, 33, 41, 54)),
+    (1, 1, (9, 12, 19, 24, 28, 33, 40, 54)),
     (1, 2, (29, 34, 38, 43, 47, 50, 55, 59)),
-    (0, 1, (19, 25, 31, 37, 44, 48, 53, 58)),
-    (0, 2, (32, 35, 42, 46, 49, 52, 57, 60)),
+    (0, 1, (20, 25, 31, 37, 44, 48, 53, 58)),
+    (0, 2, (32, 35, 41, 46, 49, 52, 57, 60)),
 )
 
 

time: 90.2 us -> 89.4 us (level)
  no operation moved by 1% of the time
where the time goes in v7:
time: 89.4 us; the launch traced here: 89.3 us
  Pallas kernels  87.4 us (98%)
  other arithmetic  1.24 us (1%)
    pallas_call x1, Pallas kernels, body(): pl.pallas_call(functools.partial(kernel, rows, total), out_shape=(pltpu.V...  87.4 us

profile of v7, /device:TPU:1, one launch (start us, length us, event | category | flops | bytes accessed | tf_op | source)
XLA Modules:
  0.0 89.3 jit_solution(3946056546758076384)
XLA Ops:
  0.6 87.4 %gram_gradient.1 = (f32[512,512]{1,0:T(8,128)S(1)}, f32[512,512]{1,0:T(8,128)S(1)}, f32[8,512]{1,0:T(8,128)S(1)}) custom-call(bf16[512,512]{1,0:T(8,128)(2,1)} %far_a.1, bf16[512,512]{1,0:T(8,128)(2,1)} %far_b.1), custom_call_target="tpu_custom_call" | custom-call | tf_op jit(solution)/shard_map/gram_gradient/pallas_call | solution.py:552
  88.0 1.2 %multiply_convert_fusion = (bf16[512,512]{1,0:T(8,128)(2,1)}, bf16[512,512]{1,0:T(8,128)(2,1)}) fusion(f32[512,512]{1,0:T(8,128)S(1)} %get-tuple-element.7, f32[512]{0:T(512)S(1)} %bitcast.2, f32[512,512]{1,0:T(8,128)S(1)} %get-tuple-element.6, f32[512]{0:T(512)S(1)} %bitcast.3), kind=kLoop, calls=%fused_computation | loop fusion | flops 1048576 | bytes 3149824 | tf_op jit(solution)/shard_map/convert_element_type | solution.py:578
  (1 shorter events, 0.0 us)

commit v8 on v7

--- a/solution.py
+++ b/solution.py
@@ -62,9 +62,10 @@
     pltpu.make_async_copy(moved, moved, sem).wait()
 
 
-def kernel(rows, total, far_a, far_b, ga, gb, moments, *scratch):
-    (raw, normed, stat, same, last_a, last_b, acc, cross, back, own, own_sems, send_sems, recv_sems) = scratch[:13]
+def kernel(rows, total, far_a, far_b, acc_a, acc_b, moments, sums_ab, *scratch):
+    (raw, normed, stat, same, last_a, last_b, cross, mirror, own, row_sums, own_sems, send_sems, recv_sems) = scratch[:13]
     blocks = scratch[13:]
+    acc = (acc_a, acc_b)
     net = Net(send_sems, recv_sems)
     views = (own.at[0], own.at[1])
     loads = [
@@ -85,7 +86,7 @@
         return (batch, rem4(y + dy) * 4 + rem4(z + dz))
 
     peers = [(lax.rem(batch + k, 8), feat) for k in (4, 3, 5, 2, 6, 1, 7)]
-    planes = [at_feat(half, k, 0) for half in range(2) for k in range(1, 4)]
+    planes = [at_feat(half, k, 0) for half in range(2) for k in (2, 1, 3)]
     barrier = pltpu.get_barrier_semaphore()
     for device in peers + planes:
         pl.semaphore_signal(barrier, inc=1, device_id=device, device_id_type=MESH)
@@ -194,8 +195,9 @@
         normalize(v, 5)
 
     net.cross_sends = [net.sender(cross.at[v]) for v in range(2)]
-    net.back_sends = [net.sender(back.at[v]) for v in range(2)]
-    begun = set()
+    net.back_sends = [net.sender(mirror.at[v]) for v in range(2)]
+    added = [0, 0]
+    row_sums[...] = jnp.zeros((2, 8, rows), F32)
 
     def cross_rows(part, turn):
         return pl.ds(pl.multiple_of(lax.rem(part + turn, 2) * 256, 256), 256)
@@ -214,14 +216,21 @@
         )
 
     def add(v, here, value):
-        acc[v, here, :] = acc[v, here, :] + value if v in begun else value
+        if added[v] < 3 or v == 0:
+            acc[v][here, :] = acc[v][here, :] + value if added[v] else value
+            return
+        back = (2.0 * LAMBDA / total) * (acc[v][here, :] + value)
+        back += extras[0] * normed[1 - v, 0, here, :].astype(F32)
+        acc[v][here, :] = back
+        row_sums[0] += jnp.sum(back.reshape(-1, 8, rows), axis=0)
+        row_sums[1] += jnp.sum((back * unit_of(v, here)).reshape(-1, 8, rows), axis=0)
 
     class Block:
         def __init__(self, v, kind):
             self.v, self.kind = v, kind
             base = (v * 3 + kind) * 5
             self.part, self.r1, self.r2, self.r3, self.full = blocks[base : base + 5]
-            self.cross, self.back = cross.at[v], back.at[v]
+            self.cross, self.back = cross.at[v], mirror.at[v]
             self.columns = REDUCED[kind]
             mirrored = 1 if kind == 2 else 0
             self.reduce_send = net.sender(self.part.at[pl.ds(0, 30)])
@@ -418,7 +427,7 @@
                         value += mirrored(left, normed[other, 5 - turned])
                     add(other, here, value)
 
-            begun.add(other)
+            added[other] += 1
 
         def apply_own(self, other):
             @pl.loop(0, rows // 128)
@@ -455,7 +464,7 @@
                 value += mirrored(self.back[1, :, :, here], normed[other, 3])
                 add(other, here, value)
 
-            begun.add(other)
+            added[other] += 1
 
         def stages(self):
             reduce = [self.product, self.pass_on, self.turn, self.reduced]
@@ -485,27 +494,24 @@
     def back_sums(v, last):
         def step_sum(step, carry):
             here = pl.ds(pl.multiple_of(step * 64, 64), 64)
-            back = (2.0 * LAMBDA / total) * acc[v, here, :]
+            back = (2.0 * LAMBDA / total) * acc[v][here, :]
             back += extras[0] * normed[1 - v, 0, here, :].astype(F32)
-            acc[v, here, :] = back
+            acc[v][here, :] = back
             first = carry[0] + jnp.sum(back.reshape(8, 8, -1), axis=0)
             second = carry[1] + jnp.sum((back * unit_of(v, here)).reshape(8, 8, -1), axis=0)
             return first, second
 
         first, second = lax.fori_loop(0, rows // 64, step_sum, (zero, zero))
+        return send_sums(first, second, last)
+
+    def send_sums(first, second, last):
         last[batch, pl.ds(0, 1), :] = jnp.sum(first, axis=0, keepdims=True)
         last[batch, pl.ds(1, 1), :] = jnp.sum(second, axis=0, keepdims=True)
         last[batch, pl.ds(2, 6), :] = jnp.zeros((6, rows), F32)
         return exchange(last, 2)
 
-    def finish(v, last, items, out):
-        both = collect(last, items, 2) / total
-        first, second = both[0:1], both[1:2]
-
-        @pl.loop(0, rows // 64)
-        def _(step):
-            here = pl.ds(pl.multiple_of(step * 64, 64), 64)
-            out[here, :] = acc[v, here, :] - first - unit_of(v, here) * second
+    def finish(v, last, items):
+        sums_ab[pl.ds(2 * v, 2), :] = (collect(last, items, 2) / total)[0:2]
 
     plan = []
 
@@ -528,9 +534,11 @@
     add_rows([early], (max(ticks[-1] for v, _, ticks in BLOCKS if v == 1),))
     for _, step in sorted(plan, key=lambda item: item[0]):
         step()
-    items_b = back_sums(1, last_b)
-    finish(0, last_a, extras[1], ga)
-    finish(1, last_b, items_b, gb)
+    assert added == [4, 4]
+    items_b = send_sums(row_sums[0], row_sums[1], last_b)
+    sums_ab[pl.ds(4, 4), :] = jnp.zeros((4, rows), F32)
+    finish(0, last_a, extras[1])
+    finish(1, last_b, items_b)
     net.finish()
     assert (len(net.sends), net.receives) == (SENDS, RECEIVES)
 
@@ -549,11 +557,11 @@
                 pltpu.VMEM((32, 16, wide), BF16),
             ]
     vmem = pl.BlockSpec(memory_space=pltpu.VMEM)
-    left_a, left_b, moments = pl.pallas_call(
+    back_a, back_b, moments, sums = pl.pallas_call(
         functools.partial(kernel, rows, total),
-        out_shape=(pltpu.VMEM((rows, width), F32),) * 2 + (pltpu.VMEM((8, width), F32),),
+        out_shape=(pltpu.VMEM((rows, width), F32),) * 2 + (pltpu.VMEM((8, width), F32),) * 2,
         in_specs=[pl.BlockSpec(memory_space=pl.ANY)] * 2,
-        out_specs=(vmem, vmem, vmem),
+        out_specs=(vmem,) * 4,
         scratch_shapes=[
             pltpu.VMEM((2, 8, rows, width), BF16),
             pltpu.VMEM((2, 8, rows, width), BF16),
@@ -561,10 +569,10 @@
             pltpu.VMEM((8, 8, width), F32),
             pltpu.VMEM((8, 8, width), F32),
             pltpu.VMEM((8, 8, width), F32),
-            pltpu.VMEM((2, rows, width), F32),
             pltpu.VMEM((2, 32, 16, 256), BF16),
             pltpu.VMEM((2, 2, 32, 16, 512), BF16),
             pltpu.VMEM((2, rows, width), BF16),
+            pltpu.VMEM((2, 8, width), F32),
             pltpu.SemaphoreType.DMA((2,)),
             pltpu.SemaphoreType.DMA((SENDS,)),
             pltpu.SemaphoreType.DMA((RECEIVES,)),
@@ -575,7 +583,13 @@
         ),
         name="gram_gradient",
     )(view_a, view_b)
-    return (moments[1] * left_a).astype(BF16), (moments[3] * left_b).astype(BF16)
+
+    def gradient(v, view, back):
+        scale = moments[2 * v + 1]
+        unit = (view.astype(F32) - moments[2 * v]) * scale
+        return (scale * (back - sums[2 * v] - unit * sums[2 * v + 1])).astype(BF16)
+
+    return gradient(0, view_a, back_a), gradient(1, view_b, back_b)
 
 
 def solution(mesh):

time: 89.4 us -> 89.2 us (level)
  no operation moved by 1% of the time
where the time goes in v8:
time: 89.2 us; the launch traced here: 89.1 us
  Pallas kernels  86.9 us (97%)
  other arithmetic  1.51 us (2%)
    pallas_call x1, Pallas kernels, body(): pl.pallas_call(functools.partial(kernel, rows, total), out_shape=(pltpu.V...  86.9 us

profile of v8, /device:TPU:1, one launch (start us, length us, event | category | flops | bytes accessed | tf_op | source)
XLA Modules:
  0.0 89.1 jit_solution(1369203801169559362)
XLA Ops:
  0.6 0.0 copy-start
  0.6 0.0 copy-start.1
  0.6 86.9 %gram_gradient.1 = (f32[512,512]{1,0:T(8,128)S(1)}, f32[512,512]{1,0:T(8,128)S(1)}, f32[8,512]{1,0:T(8,128)S(1)}, f32[8,512]{1,0:T(8,128)S(1)}) custom-call(bf16[512,512]{1,0:T(8,128)(2,1)} %far_a.1, bf16[512,512]{1,0:T(8,128)(2,1)} %far_b.1), custom_call_target="tpu_custom_call" | custom-call | tf_op jit(solution)/shard_map/gram_gradient/pallas_call | solution.py:560
  87.6 0.0 copy-done
  87.6 0.0 copy-done.1
  87.6 1.5 %multiply_convert_fusion = (bf16[512,512]{1,0:T(8,128)(2,1)}, bf16[512,512]{1,0:T(8,128)(2,1)}) fusion(bf16[512,512]{1,0:T(8,128)(2,1)S(1)} %copy-done, f32[512,512]{1,0:T(8,128)S(1)} %get-tuple-element.9, f32[512]{0:T(512)S(1)} %bitcast.13, f32[512]{0:T(512)S(1)} %bitcast.9, f32[512]{0:T(512)S(1)} %bitcast.12, f32[512]{0:T(512)S(1)} %bitcast.8, ...), kind=kLoop, calls=%fused_computation | loop fusion | flops 4194304 | bytes 4210688 | tf_op jit(solution)/shard_map/convert_element_type | solution.py:590
  (2 shorter events, 0.0 us)
Async XLA Ops:
  0.6 86.9 %copy-start = (bf16[512,512]{1,0:T(8,128)(2,1)S(1)}, bf16[512,512]{1,0:T(8,128)(2,1)}, u32[]{:S(2)}) copy-start(bf16[512,512]{1,0:T(8,128)(2,1)} %far_b.1) | copy-start | bytes 1572868
  0.6 86.9 %copy-start.1 = (bf16[512,512]{1,0:T(8,128)(2,1)S(1)}, bf16[512,512]{1,0:T(8,128)(2,1)}, u32[]{:S(2)}) copy-start(bf16[512,512]{1,0:T(8,128)(2,1)} %far_a.1) | copy-start | bytes 1572868

commit v9 on v7

--- a/solution.py
+++ b/solution.py
@@ -233,23 +233,25 @@
 
         def product(self):
             v = self.v
-            @pl.loop(0, rows // 128)
+            @pl.loop(0, 2)
             def _(step):
-                left = normed[v, 0, pl.ds(pl.multiple_of(step * 128, 128), 128), :]
-
-                def block(first, right):
+                def block(first, right, tile_rows=256, part=0):
+                    start = pl.multiple_of(step * 256 + part * 128, 128)
+                    left = normed[v, 0, pl.ds(start, tile_rows), :]
                     value = lax.dot_general(
                         left, right, (((1,), (1,)), ((), ())), preferred_element_type=F32
                     )
                     width = right.shape[0]
-                    self.part[pl.ds(step * 8, 8), :, pl.ds(first, width)] = value.astype(
-                        BF16
-                    ).reshape(8, 16, width)
+                    chunks = pl.ds(step * 16 + part * 8, tile_rows // 16)
+                    self.part[chunks, :, pl.ds(first, width)] = value.astype(BF16).reshape(
+                        tile_rows // 16, 16, width
+                    )
 
                 if self.kind == 0:
-                    block(0, normed[v, 0, cross_rows(step // 2, 0), :])
-                    block(256, normed[v, 0, tile(partner(step)), :])
-                    block(384, normed[v, 1, cross_rows(step // 2, core), :])
+                    block(0, normed[v, 0, cross_rows(step, 0), :])
+                    for part in range(2):
+                        block(256, normed[v, 0, tile(partner(step * 2 + part)), :], 128, part)
+                    block(384, normed[v, 1, cross_rows(step, core), :])
                 elif self.kind == 1:
                     block(0, normed[v, 2])
                     block(rows, normed[v, 7])

time: 89.4 us -> 90 us (level)
  no operation moved by 1% of the time
where the time goes in v9:
time: 90 us; the launch traced here: 89.9 us
  Pallas kernels  88 us (98%)
  other arithmetic  1.24 us (1%)
    pallas_call x1, Pallas kernels, body(): pl.pallas_call(functools.partial(kernel, rows, total), out_shape=(pltpu.V...  88 us

profile of v9, /device:TPU:1, one launch (start us, length us, event | category | flops | bytes accessed | tf_op | source)
XLA Modules:
  0.0 89.9 jit_solution(1509850095087381026)
XLA Ops:
  0.6 88.0 %gram_gradient.1 = (f32[512,512]{1,0:T(8,128)S(1)}, f32[512,512]{1,0:T(8,128)S(1)}, f32[8,512]{1,0:T(8,128)S(1)}) custom-call(bf16[512,512]{1,0:T(8,128)(2,1)} %far_a.1, bf16[512,512]{1,0:T(8,128)(2,1)} %far_b.1), custom_call_target="tpu_custom_call" | custom-call | tf_op jit(solution)/shard_map/gram_gradient/pallas_call | solution.py:554
  88.7 1.2 %multiply_convert_fusion = (bf16[512,512]{1,0:T(8,128)(2,1)}, bf16[512,512]{1,0:T(8,128)(2,1)}) fusion(f32[512,512]{1,0:T(8,128)S(1)} %get-tuple-element.7, f32[512]{0:T(512)S(1)} %bitcast.2, f32[512,512]{1,0:T(8,128)S(1)} %get-tuple-element.6, f32[512]{0:T(512)S(1)} %bitcast.3), kind=kLoop, calls=%fused_computation | loop fusion | flops 1048576 | bytes 3149824 | tf_op jit(solution)/shard_map/convert_element_type | solution.py:580
  (1 shorter events, 0.0 us)
